TPU v7x, 512 devices: a whole 4x4x16 slice. The times are simulated.
512 devices in a mesh: wide: 16 (over x, z_hi), long: 32 (over z_lo, y, core).
Axes of the slice: x: 4, y: 4, z: 16 (z_hi: 4, z_lo: 4; z = z_hi * 4 + z_lo), core: 2. Of those that a mesh axis runs over, the one named last changes fastest.
Arguments:
- velocity: bfloat16 [3, 128, 1024, 512], P(None, 'wide', 'long'), may hold values from -6 to 6
- vorticity: bfloat16 [3, 128, 1024, 512], P(None, 'wide', 'long'), may hold values from -6 to 6
- m_of_slot: int32 [512], replicated, may hold values from 0 to 511, as said below
- legendre: bfloat16 [512, 512, 512], P('long', 'wide'), as said below
- known_term: bfloat16 [512, 2, 3, 512, 128], P('long', None, None, 'wide'), may hold values from -6 to 6
- inverse: bfloat16 [512, 128, 128], P('wide'), may hold values from -0.5 to 0.5
Outputs:
- section_state: bfloat16 [512, 2, 3, 512, 128], P('long', None, None, 'wide')
Inputs may be any that keep to these rules, and one draw needn't show every extreme that they name: m_of_slot is a permutation of 0 to 511; the m of slot s differs from s by less than 32. legendre[s, l, t] is zero wherever the degree l is below m_of_slot[s].
All inputs are finite; a program needn't handle non-finite values.
Results may differ from a plain program's by a relative error of at most 0.0059.
Values may be sent and summed in bfloat16 or wider, within the bound.
No kernel may reach another device: no remote copies, remote signals or barrier semaphores. Data moves between devices by JAX's collectives and lax.ppermute only.
A program may use at most 192 MiB of HBM per device.

v0:
```python
import math

import jax
import jax.numpy as jnp
from jax import lax
from jax.sharding import PartitionSpec as P

section_step = 0.75


def lamb_product(velocity, vorticity):
    vel = velocity.astype(jnp.float32)
    vort = vorticity.astype(jnp.float32)
    first = vel[1] * vort[2] - vel[2] * vort[1]
    second = vel[2] * vort[0] - vel[0] * vort[2]
    third = vel[0] * vort[1] - vel[1] * vort[0]
    return jnp.stack([first, second, third], axis=0).astype(jnp.bfloat16)


def phase_table(m_of_slot, points):
    column = jnp.arange(points, dtype=jnp.int32)
    paired_modes = jnp.repeat(m_of_slot, 2)
    parity = jnp.arange(paired_modes.shape[0], dtype=jnp.int32) % 2
    product = column[:, None] * paired_modes[None, :] % points
    phase_angle = 2.0 * math.pi / points * product.astype(jnp.float32)
    norm_factor = math.sqrt(2.0 / points)
    values = jnp.where(
        parity[None, :] == 0,
        norm_factor * jnp.cos(phase_angle),
        -norm_factor * jnp.sin(phase_angle),
    )
    return values.astype(jnp.bfloat16)


def body(velocity, vorticity, m_of_slot, legendre, known_term, inverse):
    lamb_vector = lamb_product(velocity, vorticity)
    full_phi = lax.all_to_all(lamb_vector, "long", split_axis=3, concat_axis=2, tiled=True)
    table_local = phase_table(m_of_slot, full_phi.shape[2])
    fourier = jnp.einsum(
        "frjt,jc->frct", full_phi, table_local, preferred_element_type=jnp.float32
    ).astype(jnp.bfloat16)
    slot_major = lax.all_to_all(fourier, "long", split_axis=2, concat_axis=3, tiled=True)
    slot_count = legendre.shape[0]
    nodes = slot_major.shape[3]
    piece = lax.all_gather(slot_major, "wide", axis=1, tiled=True)
    piece_block = piece.reshape(3, piece.shape[1], slot_count, 2, nodes)
    summed = jnp.einsum(
        "frsct,slt->scflr", piece_block, legendre, preferred_element_type=jnp.float32
    )
    coeffs = summed.astype(jnp.bfloat16)
    coeffs = lax.optimization_barrier(coeffs)
    right_side = (
        known_term.astype(jnp.float32) + section_step * coeffs.astype(jnp.float32)
    ).astype(jnp.bfloat16)
    solved = jnp.einsum("scflr,lqr->scflq", right_side, inverse, preferred_element_type=jnp.float32)
    return solved.astype(jnp.bfloat16)


def solution(mesh):
    return jax.shard_map(
        body,
        mesh=mesh,
        in_specs=(
            P(None, "wide", "long", None),
            P(None, "wide", "long", None),
            P(),
            P("long", "wide", None),
            P("long", None, None, "wide", None),
            P("wide", None, None),
        ),
        out_specs=P("long", None, None, "wide", None),
        check_vma=False,
    )
```

profile of v0, /device:TPU:1, one launch (start us, length us, event | category | flops | bytes accessed | tf_op | source)
XLA Modules:
  0.0 1266.5 jit_solution(17308692861983787634)
XLA Ops:
  6.5 0.0 copy-start
  6.5 1.4 convert_element_type.43
  8.0 1.3 convert_element_type.44
  9.3 0.5 subtract_convert_fusion.2
  9.8 0.1 pad_maximum_fusion
  9.9 0.0 copy-start.3
  9.9 3.6 copy.24
  13.5 5.8 reshape.19
  19.3 10.4 all-to-all-start
  29.7 0.2 all-gather.2.cloned.1.call-start
  29.9 0.0 copy-done.3
  30.0 0.1 broadcast_in_dim.14
  30.1 0.2 mul.64
  30.3 21.1 %all-to-all-done = bf16[32,2,6144]{2,1,0:T(2,128)(2,1)S(1)} async-done(((bf16[32,2,6144]{2,1,0:T(2,128)(2,1)}), bf16[32,2,6144]{2,1,0:T(2,128)(2,1)S(1)}, u32[]{:S(2)}, u32[]{:S(2)}) %all-to-all-start) | async-done | bytes 786464 | tf_op jit(solution)/shard_map/all_to_all | solution.py:37
  51.4 2.7 reshape.20
  54.0 5.6 copy.26
  59.6 4.8 all_to_all.29
  64.5 17.9 %fusion.20 = bf16[3,8,1024,16]{2,3,1,0:T(8,128)(2,1)S(1)} fusion(bf16[3,8,1024,16]{2,3,1,0:T(8,128)(2,1)S(1)} %all_to_all.29, s32[1024]{0:T(1024)S(1)} %mul.64, pred[1024]{0:T(1024)(128)(4,1)S(1)} %fusion.28), kind=kOutput, calls=%fused_computation.24 | convolution fusion | flops 824573952 | bytes 1577984 | tf_op jit(solution)/shard_map/frjt,jc->frct/dot_general | solution.py:39
  82.3 6.1 copy.27
  88.4 8.9 reshape.21
  97.3 25.9 %all_to_all.36 = bf16[32,2,6144]{2,1,0:T(2,128)(2,1)S(1)} all-to-all(bf16[32,2,6144]{2,1,0:T(2,128)(2,1)S(1)} %reshape.21), channel_id=1, replica_groups=mesh['wide'=16,'long'=32] {'long'}, dimensions={0} | all-to-all | bytes 1572864 | tf_op jit(solution)/shard_map/all_to_all | solution.py:42
  123.2 5.6 reshape.22
  128.8 7.7 copy.28
  136.5 0.0 all-gather.2.cloned.1.call-update
  136.5 0.0 copy-start.2
  136.5 1068.2 %all-gather.2.cloned.1.call-done = bf16[3,128,32,512]{2,3,1,0:T(8,128)(2,1)} async-done(((bf16[3,8,32,512]{2,3,1,0:T(8,128)(2,1)}), bf16[3,128,32,512]{2,3,1,0:T(8,128)(2,1)}) %all-gather.2.cloned.1.call-update) | async-done | bytes 12582928 | tf_op jit(solution)/shard_map/all_gather | solution.py:45
  1204.7 45.8 %copy.37 = bf16[3,128,32,512]{3,1,0,2:T(8,128)(2,1)} copy(bf16[3,128,32,512]{2,3,1,0:T(8,128)(2,1)} %all-gather.2.cloned.1.call-done) | data formatting | bytes 25165824 | tf_op jit(solution)/shard_map/reshape | solution.py:46
  1250.5 0.0 copy-done.2
  1250.6 6.8 fusion.24
  1257.4 0.3 add_convert_fusion
  1257.7 0.8 fusion.23
  1258.5 1.2 copy.32
  (4 shorter events, 0.0 us)
Async XLA Ops:
  6.5 1251.2 %copy-start = (bf16[32,128,128]{2,1,0:T(8,128)(2,1)S(1)}, bf16[32,128,128]{2,1,0:T(8,128)(2,1)}, u32[]{:S(2)}) copy-start(bf16[32,128,128]{2,1,0:T(8,128)(2,1)} %param.11) | copy-start | bytes 3145732
  9.9 20.1 %copy-start.3 = (s32[512]{0:T(512)S(1)}, s32[512]{0:T(512)}, u32[]{:S(2)}) copy-start(s32[512]{0:T(512)} %param.8) | copy-start | bytes 6148
  19.3 32.1 %all-to-all-start = ((bf16[32,2,6144]{2,1,0:T(2,128)(2,1)}), bf16[32,2,6144]{2,1,0:T(2,128)(2,1)S(1)}, u32[]{:S(2)}, u32[]{:S(2)}) async-start(bf16[32,2,6144]{2,1,0:T(2,128)(2,1)} %reshape.19), calls=%async_computation | async-start | bytes 1572864 | tf_op jit(solution)/shard_map/all_to_all | solution.py:37
  29.7 1175.0 %all-gather.2.cloned.1.call-start = ((), (), s32[]{:S(2)}) async-start(), calls=%async_computation.2 | async-start | bytes 53477376 | tf_op jit(solution)/shard_map/all_gather | solution.py:45
  136.5 1114.0 %copy-start.2 = (bf16[16,32,512]{2,1,0:T(8,128)(2,1)S(1)}, bf16[16,32,512]{2,1,0:T(8,128)(2,1)}, u32[]{:S(2)}) copy-start(bf16[16,32,512]{2,1,0:T(8,128)(2,1)} %param.9) | copy-start | bytes 1572868
  1250.5 6.9 copy-start.1
Sparse Core Ops, SparseCore 0:
  136.6 1068.0 all-gather.1
where the time goes:
time: 1270 us
  waiting for transfers between devices  1090 us (86%)
  local copies, waits for them, and re-layouts  98.1 us (8%)
  blocking collectives  25.9 us (2%)
  matrix products  25.5 us (2%)
  between operations  13.5 us (1%)
    all_gather x1, waiting for transfers between devices, body(): piece = lax.all_gather(slot_major, 'wide', axis=1, tiled=True)  1070 us
    reshape x1, local copies, waits for them, and re-layouts, body(): piece_block = piece.reshape(3, piece.shape[1], slot_count, 2, nodes)  45.8 us
    all_to_all x1, blocking collectives, body(): lax.all_to_all(fourier, 'long', split_axis=2, concat_axis=3, tiled=True)  25.9 us
  transfers between devices with their start and end apart: 2, of which 2 were waited for; matrix products, arithmetic and copies ran while one was open for 0% of the time, Pallas kernels for 0%

commit v1 on v0

v1 whole, which is shorter than its diff:
```python
import math

import jax
import jax.numpy as jnp
from jax import lax
from jax.experimental import pallas as pl
from jax.experimental.pallas import tpu as pltpu
from jax.sharding import PartitionSpec as P

section_step = 0.75
VMEM_LIMIT = 48 * 1024 * 1024
LANES = 128


def params():
    return pltpu.CompilerParams(vmem_limit_bytes=VMEM_LIMIT)


def lamb_kernel(vel_ref, vort_ref, out_ref):
    vel = [vel_ref[i, 0].astype(jnp.float32) for i in range(3)]
    vort = [vort_ref[i, 0].astype(jnp.float32) for i in range(3)]
    for f in range(3):
        a, b = (f + 1) % 3, (f + 2) % 3
        lamb = (vel[a] * vort[b] - vel[b] * vort[a]).astype(jnp.bfloat16)
        for tb in range(lamb.shape[1] // LANES):
            out_ref[tb, f] = lamb[:, tb * LANES : (tb + 1) * LANES]


def lamb_blocks(velocity, vorticity):
    _, nr, nj, nt = velocity.shape
    tbs = nt // LANES
    spec = pl.BlockSpec((3, 1, nj, nt), lambda r: (0, r, 0, 0))
    return pl.pallas_call(
        lamb_kernel,
        grid=(nr,),
        in_specs=[spec, spec],
        out_specs=pl.BlockSpec((tbs, 3, nj, LANES), lambda r: (r, 0, 0, 0)),
        out_shape=jax.ShapeDtypeStruct((nr * tbs, 3, nj, LANES), jnp.bfloat16),
        compiler_params=params(),
    )(velocity, vorticity)


def phase_rows(m_of_slot, points, subs):
    modes = m_of_slot.reshape(-1, subs).T.reshape(-1)
    paired = jnp.repeat(modes, 2)
    parity = jnp.arange(paired.shape[0], dtype=jnp.int32) % 2
    column = jnp.arange(points, dtype=jnp.int32)
    product = (paired[:, None] * column[None, :] + parity[:, None] * (points // 4)) % points
    angle = 2.0 * math.pi / points * product.astype(jnp.float32)
    return (math.sqrt(2.0 / points) * jnp.cos(angle)).astype(jnp.bfloat16)


def dft_kernel(x_ref, table_ref, out_ref):
    points = table_ref.shape[1]
    grid = jnp.concatenate([x_ref[:, f].reshape(points, LANES) for f in range(3)], axis=1)
    out_ref[...] = jnp.dot(table_ref[...], grid, preferred_element_type=jnp.float32).astype(jnp.bfloat16)


def dft(x, table):
    rows, points = table.shape
    step = 256
    return pl.pallas_call(
        dft_kernel,
        grid=(rows // step,),
        in_specs=[
            pl.BlockSpec(x.shape, lambda i: (0, 0, 0, 0)),
            pl.BlockSpec((step, points), lambda i: (i, 0)),
        ],
        out_specs=pl.BlockSpec((step, 3 * LANES), lambda i: (i, 0)),
        out_shape=jax.ShapeDtypeStruct((rows, 3 * LANES), jnp.bfloat16),
        compiler_params=params(),
    )(x, table)


def reorder(source_of, n):
    row = lax.broadcasted_iota(jnp.int32, (n, n), 0)
    column = lax.broadcasted_iota(jnp.int32, (n, n), 1)
    return (source_of(row) == column).astype(jnp.float32).astype(jnp.bfloat16)


def legendre_kernel(y_ref, leg_ref, out_ref, side):
    blocks = y_ref.shape[0] // 256
    nodes = side.shape[1]
    tbs = nodes // LANES
    per = 256 // (2 * tbs)

    def source(i):
        tb, rest = i // (2 * per), i % (2 * per)
        c, wr = rest // per, rest % per
        return (wr * tbs + tb) * 2 + c

    move = reorder(source, 256)
    half = side.shape[0] // 2
    for k in range(blocks):
        moved = jnp.dot(
            move, y_ref[k * 256 : (k + 1) * 256, :], preferred_element_type=jnp.float32
        ).astype(jnp.bfloat16)
        for tb in range(tbs):
            for c in range(2):
                start = (tb * 2 + c) * per
                side[c * half + k * per : c * half + (k + 1) * per, tb * LANES : (tb + 1) * LANES] = (
                    moved[start : start + per, :]
                )
    coeffs = lax.dot_general(
        leg_ref[...], side[...], (((1,), (1,)), ((), ())), preferred_element_type=jnp.float32
    ).astype(jnp.bfloat16)
    wides, degrees = out_ref.shape[0], out_ref.shape[3]
    for c in range(2):
        out_ref[:, c, 0] = coeffs[:, c * half : (c + 1) * half].reshape(wides, degrees, half)


def legendre_step(y, leg, wides):
    rows = y.shape[0]
    degrees, nodes = leg.shape
    tbs = nodes // LANES
    nr = rows // (2 * tbs)
    return pl.pallas_call(
        legendre_kernel,
        grid=(3,),
        in_specs=[
            pl.BlockSpec((rows, LANES), lambda f: (0, f)),
            pl.BlockSpec(leg.shape, lambda f: (0, 0)),
        ],
        out_specs=pl.BlockSpec((wides, 2, 1, degrees // wides, nr), lambda f: (0, 0, f, 0, 0)),
        out_shape=jax.ShapeDtypeStruct((wides, 2, 3, degrees // wides, nr), jnp.bfloat16),
        scratch_shapes=[pltpu.VMEM((2 * nr, nodes), jnp.bfloat16)],
        compiler_params=params(),
    )(y, leg)


def solve_kernel(coeffs_ref, known_ref, inverse_ref, out_ref, side, solved):
    lines, degrees, nr = coeffs_ref.shape
    swap = reorder(lambda i: (i % 16) * 16 + i // 16, 256)
    for a in range(lines // 16):
        for h in range(degrees // 16):
            here = (slice(a * 16, (a + 1) * 16), slice(h * 16, (h + 1) * 16))
            right = (
                known_ref[here].astype(jnp.float32) + section_step * coeffs_ref[here].astype(jnp.float32)
            ).astype(jnp.bfloat16)
            moved = jnp.dot(swap, right.reshape(256, nr), preferred_element_type=jnp.float32)
            side[here[1], here[0]] = moved.astype(jnp.bfloat16).reshape(16, 16, nr)
    for k in range(degrees):
        solved[k] = lax.dot_general(
            side[k], inverse_ref[k], (((1,), (1,)), ((), ())), preferred_element_type=jnp.float32
        ).astype(jnp.bfloat16)
    for a in range(lines // 16):
        for h in range(degrees // 16):
            here = (slice(a * 16, (a + 1) * 16), slice(h * 16, (h + 1) * 16))
            moved = jnp.dot(
                swap, solved[here[1], here[0]].reshape(256, nr), preferred_element_type=jnp.float32
            )
            out_ref[here] = moved.astype(jnp.bfloat16).reshape(16, 16, nr)


def radial_solve(coeffs, known, inverse):
    lines, degrees, nr = coeffs.shape
    return pl.pallas_call(
        solve_kernel,
        out_shape=jax.ShapeDtypeStruct(coeffs.shape, jnp.bfloat16),
        scratch_shapes=[pltpu.VMEM((degrees, lines, nr), jnp.bfloat16)] * 2,
        compiler_params=params(),
    )(coeffs, known, inverse)


def body(velocity, vorticity, m_of_slot, legendre, known_term, inverse):
    slots, degrees, nodes = legendre.shape
    wides = slots
    leg = lax.all_to_all(legendre, "wide", split_axis=0, concat_axis=0, tiled=True)
    leg = leg.reshape(wides * degrees, nodes)
    blocks = lamb_blocks(velocity, vorticity)
    blocks = lax.all_to_all(blocks, "long", split_axis=0, concat_axis=0, tiled=True)
    blocks, leg = lax.optimization_barrier((blocks, leg))
    points = blocks.shape[0] * blocks.shape[2]
    table = phase_rows(m_of_slot, points, slots)
    fourier = dft(blocks, table)
    fourier = fourier.reshape(-1, 2, 3 * LANES)
    fourier = lax.all_to_all(fourier, ("wide", "long"), split_axis=0, concat_axis=0, tiled=True)
    coeffs = legendre_step(fourier.reshape(-1, 3 * LANES), leg, wides)
    coeffs = lax.all_to_all(coeffs, "wide", split_axis=0, concat_axis=0, tiled=True)
    lines = slots * 6
    solved = radial_solve(
        coeffs.reshape(lines, degrees, -1), known_term.reshape(lines, degrees, -1), inverse
    )
    return solved.reshape(known_term.shape)


def solution(mesh):
    return jax.shard_map(
        body,
        mesh=mesh,
        in_specs=(
            P(None, "wide", "long", None),
            P(None, "wide", "long", None),
            P(),
            P("long", "wide", None),
            P("long", None, None, "wide", None),
            P("wide", None, None),
        ),
        out_specs=P("long", None, None, "wide", None),
        check_vma=False,
    )
```

time: 1270 us -> 193 us (0.15)
  the two profiles are of different devices: /device:TPU:1 before, /device:TPU:32 now
where the time goes in v1:
time: 193 us
  blocking collectives  105 us (54%)
  waiting for transfers between devices  31.2 us (16%)
  starting transfers between devices  23.3 us (12%)
  other arithmetic  17.6 us (9%)
  Pallas kernels  9.38 us (5%)
  local copies, waits for them, and re-layouts  6.13 us (3%)
    all_to_all x1, blocking collectives, body(): lax.all_to_all(fourier, ('wide', 'long'), split_axis=0, concat_axis=0, ti...  55.9 us
    all_to_all x1, blocking collectives, body(): lax.all_to_all(coeffs, 'wide', split_axis=0, concat_axis=0, tiled=True)  49 us
    all_to_all x1, waiting for transfers between devices, body(): lax.all_to_all(legendre, 'wide', split_axis=0, concat_axis=0, tiled=True)  28.9 us
    convert_element_type x1, other arithmetic, phase_rows(): return (math.sqrt(2.0 / points) * jnp.cos(angle)).astype(jnp.bfloat16)  17.6 us
    all_to_all x1, starting transfers between devices, body(): lax.all_to_all(legendre, 'wide', split_axis=0, concat_axis=0, tiled=True)  16.8 us
    all_to_all x1, starting transfers between devices, body(): lax.all_to_all(blocks, 'long', split_axis=0, concat_axis=0, tiled=True)  6.52 us
  transfers between devices with their start and end apart: 2, of which 2 were waited for; matrix products, arithmetic and copies ran while one was open for 9% of the time, Pallas kernels for 2%

profile of v1, /device:TPU:32, one launch (start us, length us, event | category | flops | bytes accessed | tf_op | source)
XLA Modules:
  0.0 192.6 jit_solution(4393014371729599215)
XLA Ops:
  0.0 16.8 %all-to-all-start.1 = ((bf16[16,32,512]{2,1,0:T(8,128)(2,1)}), bf16[16,32,512]{2,1,0:T(8,128)(2,1)S(1)}, u32[]{:S(2)}, u32[]{:S(2)}) async-start(bf16[16,32,512]{2,1,0:T(8,128)(2,1)} %param.9), calls=%async_computation.1 | async-start | bytes 1048576 | tf_op jit(solution)/shard_map/all_to_all | solution.py:168
  16.8 0.0 copy-start.2
  16.8 1.1 copy-done.2
  17.9 0.0 copy-start.3
  17.9 1.1 copy-done.3
  19.0 0.0 copy-start.5
  19.0 2.9 %shard_map.64 = bf16[32,3,32,128]{3,2,1,0:T(8,128)(2,1)} custom-call(bf16[3,8,32,512]{3,2,1,0:T(8,128)(2,1)S(1)} %copy-done.2, bf16[3,8,32,512]{3,2,1,0:T(8,128)(2,1)S(1)} %copy-done.3), custom_call_target="tpu_custom_call" | custom-call | tf_op jit(solution)/shard_map/pallas_call | solution.py:33
  22.0 28.9 %all-to-all-done.1 = bf16[16,32,512]{2,1,0:T(8,128)(2,1)S(1)} async-done(((bf16[16,32,512]{2,1,0:T(8,128)(2,1)}), bf16[16,32,512]{2,1,0:T(8,128)(2,1)S(1)}, u32[]{:S(2)}, u32[]{:S(2)}) %all-to-all-start.1) | async-done | bytes 524320 | tf_op jit(solution)/shard_map/all_to_all | solution.py:168
  50.9 6.5 %all-to-all-start = ((bf16[32,3,32,128]{3,2,1,0:T(8,128)(2,1)}), bf16[32,3,32,128]{3,2,1,0:T(8,128)(2,1)S(1)}, u32[]{:S(2)}, u32[]{:S(2)}) async-start(bf16[32,3,32,128]{3,2,1,0:T(8,128)(2,1)} %shard_map.64), calls=%async_computation | async-start | bytes 1572864 | tf_op jit(solution)/shard_map/all_to_all | solution.py:171
  57.4 0.0 copy-done.5
  57.4 0.1 reshape.37
  57.5 0.1 copy.7
  57.6 0.1 reshape.38
  57.7 0.1 broadcast_in_dim.2
  57.8 0.2 mul.38
  58.0 17.6 %fusion.5.table_ref = bf16[1024,1024]{1,0:T(8,128)(2,1)S(1)} fusion(s32[1024]{0:T(1024)S(1)} %fusion.6, s32[1024]{0:T(1024)S(1)} %mul.38), kind=kLoop, calls=%fused_computation.8 | loop fusion | flops 17825792 | bytes 2105344 | tf_op jit(solution)/shard_map/convert_element_type | solution.py:50
  75.6 2.3 %all-to-all-done.x_ref = bf16[32,3,32,128]{3,2,1,0:T(8,128)(2,1)S(1)} async-done(((bf16[32,3,32,128]{3,2,1,0:T(8,128)(2,1)}), bf16[32,3,32,128]{3,2,1,0:T(8,128)(2,1)S(1)}, u32[]{:S(2)}, u32[]{:S(2)}) %all-to-all-start) | async-done | bytes 786464 | tf_op jit(solution)/shard_map/all_to_all | solution.py:171
  77.9 1.7 shard_map.65
  79.6 0.0 copy-start
  79.6 0.9 copy-done
  80.5 2.2 %reshape.39 = bf16[512,2,384]{2,1,0:T(2,128)(2,1)S(1)} reshape(bf16[1024,384]{1,0:T(8,128)(2,1)} %copy-done) | data formatting | bytes 1572864 | tf_op jit(solution)/shard_map/reshape | solution.py:176
  82.6 55.9 %all_to_all.20 = bf16[512,2,384]{2,1,0:T(2,128)(2,1)S(1)} all-to-all(bf16[512,2,384]{2,1,0:T(2,128)(2,1)S(1)} %reshape.39), channel_id=1, replica_groups=mesh['wide'=16,'long'=32] {'wide','long'}, dimensions={0} | all-to-all | bytes 1572864 | tf_op jit(solution)/shard_map/all_to_all | solution.py:177
  138.5 0.3 reshape.40.y_ref
  138.8 0.0 copy-start.1
  138.8 0.0 copy-start.4
  138.9 2.0 %shard_map.66 = bf16[16,2,3,32,128]{4,3,2,1,0:T(8,128)(2,1)S(1)} custom-call(bf16[1024,384]{1,0:T(8,128)(2,1)S(1)} %reshape.40.y_ref, bf16[512,512]{1,0:T(8,128)(2,1)S(1)} %bitcast.6), custom_call_target="tpu_custom_call" | custom-call | tf_op jit(solution)/shard_map/pallas_call | solution.py:117
  140.9 49.0 %all_to_all.21 = bf16[16,2,3,32,128]{4,3,2,1,0:T(8,128)(2,1)S(1)} all-to-all(bf16[16,2,3,32,128]{4,3,2,1,0:T(8,128)(2,1)S(1)} %shard_map.66), channel_id=1, replica_groups=mesh['wide'=16,'long'=32] {'wide'}, dimensions={0} | all-to-all | bytes 1572864 | tf_op jit(solution)/shard_map/all_to_all | solution.py:179
  189.9 0.0 copy-done.1
  189.9 0.0 copy-done.4
  189.9 2.7 %shard_map.67 = bf16[96,32,128]{2,1,0:T(8,128)(2,1)} custom-call(bf16[96,32,128]{2,1,0:T(8,128)(2,1)S(1)} %bitcast.5, bf16[96,32,128]{2,1,0:T(8,128)(2,1)S(1)} %bitcast.7, bf16[32,128,128]{2,1,0:T(8,128)(2,1)S(1)} %copy-done.1), custom_call_target="tpu_custom_call" | custom-call | tf_op jit(solution)/shard_map/pallas_call | solution.py:157
  (1 shorter events, 0.0 us)
Async XLA Ops:
  0.0 50.9 %all-to-all-start.1 = ((bf16[16,32,512]{2,1,0:T(8,128)(2,1)}), bf16[16,32,512]{2,1,0:T(8,128)(2,1)S(1)}, u32[]{:S(2)}, u32[]{:S(2)}) async-start(bf16[16,32,512]{2,1,0:T(8,128)(2,1)} %param.9), calls=%async_computation.1 | async-start | bytes 1048576 | tf_op jit(solution)/shard_map/all_to_all | solution.py:168
  16.8 1.1 copy-start.2
  17.9 1.1 copy-start.3
  19.0 38.4 %copy-start.5 = (s32[512]{0:T(512)S(1)}, s32[512]{0:T(512)}, u32[]{:S(2)}) copy-start(s32[512]{0:T(512)} %param.8) | copy-start | bytes 6148
  50.9 27.0 %all-to-all-start = ((bf16[32,3,32,128]{3,2,1,0:T(8,128)(2,1)}), bf16[32,3,32,128]{3,2,1,0:T(8,128)(2,1)S(1)}, u32[]{:S(2)}, u32[]{:S(2)}) async-start(bf16[32,3,32,128]{3,2,1,0:T(8,128)(2,1)} %shard_map.64), calls=%async_computation | async-start | bytes 1572864 | tf_op jit(solution)/shard_map/all_to_all | solution.py:171
  79.6 0.9 copy-start
  138.8 51.0 %copy-start.1 = (bf16[32,128,128]{2,1,0:T(8,128)(2,1)S(1)}, bf16[32,128,128]{2,1,0:T(8,128)(2,1)}, u32[]{:S(2)}) copy-start(bf16[32,128,128]{2,1,0:T(8,128)(2,1)} %inverse_ref.1) | copy-start | bytes 3145732
  138.8 51.0 %copy-start.4 = (bf16[16,2,3,32,128]{4,3,2,1,0:T(8,128)(2,1)S(1)}, bf16[16,2,3,32,128]{4,3,2,1,0:T(8,128)(2,1)}, u32[]{:S(2)}) copy-start(bf16[16,2,3,32,128]{4,3,2,1,0:T(8,128)(2,1)} %param.10) | copy-start | bytes 2359300

commit v2 on v1

v2 whole, which is shorter than its diff:
```python
import math

import jax
import jax.numpy as jnp
from jax import lax
from jax.experimental import pallas as pl
from jax.experimental.pallas import tpu as pltpu
from jax.sharding import Mesh
from jax.sharding import PartitionSpec as P

section_step = 0.75
VMEM_LIMIT = 48 * 1024 * 1024
LANES = 128


def params():
    return pltpu.CompilerParams(vmem_limit_bytes=VMEM_LIMIT)


def lamb_kernel(vel_ref, vort_ref, out_ref):
    vel = [vel_ref[i, 0].astype(jnp.float32) for i in range(3)]
    vort = [vort_ref[i, 0].astype(jnp.float32) for i in range(3)]
    for f in range(3):
        a, b = (f + 1) % 3, (f + 2) % 3
        lamb = (vel[a] * vort[b] - vel[b] * vort[a]).astype(jnp.bfloat16)
        for tb in range(lamb.shape[1] // LANES):
            out_ref[tb, f] = lamb[:, tb * LANES : (tb + 1) * LANES]


def lamb_blocks(velocity, vorticity):
    _, nr, nj, nt = velocity.shape
    tbs = nt // LANES
    spec = pl.BlockSpec((3, 1, nj, nt), lambda r: (0, r, 0, 0))
    return pl.pallas_call(
        lamb_kernel,
        grid=(nr,),
        in_specs=[spec, spec],
        out_specs=pl.BlockSpec((tbs, 3, nj, LANES), lambda r: (r, 0, 0, 0)),
        out_shape=jax.ShapeDtypeStruct((nr * tbs, 3, nj, LANES), jnp.bfloat16),
        compiler_params=params(),
    )(velocity, vorticity)


def phase_rows(m_of_slot, points, groups, subs):
    modes = m_of_slot.reshape(-1, groups, subs).transpose(1, 0, 2).reshape(-1)
    paired = jnp.repeat(modes, 2)
    parity = jnp.arange(paired.shape[0], dtype=jnp.int32) % 2
    column = jnp.arange(points, dtype=jnp.int32)
    product = (paired[:, None] * column[None, :] + parity[:, None] * (points // 4)) % points
    angle = 2.0 * math.pi / points * product.astype(jnp.float32)
    return (math.sqrt(2.0 / points) * jnp.cos(angle)).astype(jnp.bfloat16)


def dft_kernel(x_ref, table_ref, out_ref):
    points = table_ref.shape[1]
    grid = jnp.concatenate([x_ref[:, f].reshape(points, LANES) for f in range(3)], axis=1)
    out_ref[...] = jnp.dot(table_ref[...], grid, preferred_element_type=jnp.float32).astype(jnp.bfloat16)


def dft(x, table):
    rows, points = table.shape
    step = 256
    return pl.pallas_call(
        dft_kernel,
        grid=(rows // step,),
        in_specs=[
            pl.BlockSpec(x.shape, lambda i: (0, 0, 0, 0)),
            pl.BlockSpec((step, points), lambda i: (i, 0)),
        ],
        out_specs=pl.BlockSpec((step, 3 * LANES), lambda i: (i, 0)),
        out_shape=jax.ShapeDtypeStruct((rows, 3 * LANES), jnp.bfloat16),
        compiler_params=params(),
    )(x, table)


def matches(source_of, shape):
    row = lax.broadcasted_iota(jnp.int32, shape, 0)
    column = lax.broadcasted_iota(jnp.int32, shape, 1)
    return (source_of(row) == column).astype(jnp.float32).astype(jnp.bfloat16)


def moved_rows(matrix, array):
    return jnp.dot(matrix, array, preferred_element_type=jnp.float32).astype(jnp.bfloat16)


def legendre_kernel(zh_ref, y_ref, leg_ref, out_ref, side):
    zh = zh_ref[0]
    pair = pl.program_id(0)
    for kk in range(2):
        k = pair * 2 + kk

        def source(i):
            tb, c, z, r = i // 32, (i // 16) % 2, (i // 8) % 2, i % 8
            return ((z * 8 + r) * 4 + tb) * 8 + k * 2 + c

        move = matches(source, (128, 512))
        for h in range(2):
            moved = moved_rows(move, y_ref[h * 512 : (h + 1) * 512, :])
            for tb in range(4):
                for c in range(2):
                    for f in range(3):
                        start = (c * 3 + f) * 32 + h * 16
                        side[kk, start : start + 16, tb * LANES : (tb + 1) * LANES] = moved[
                            (tb * 2 + c) * 16 : (tb * 2 + c) * 16 + 16, f * LANES : (f + 1) * LANES
                        ]
    for x in range(4):
        coeffs = [
            lax.dot_general(
                leg_ref[x, kk].reshape(128, -1),
                side[kk],
                (((1,), (1,)), ((), ())),
                preferred_element_type=jnp.float32,
            ).astype(jnp.bfloat16)
            for kk in range(2)
        ]
        both = jnp.concatenate(coeffs, axis=1)
        for d in range(4):
            out_ref[x * 4 + ((zh - d) & 3), 0] = both[d * 32 : (d + 1) * 32, :]


def legendre_step(zh, y, leg):
    nodes = leg.shape[-1]
    return pl.pallas_call(
        legendre_kernel,
        grid=(2,),
        in_specs=[
            pl.BlockSpec(memory_space=pltpu.SMEM),
            pl.BlockSpec(y.shape, lambda p: (0, 0)),
            pl.BlockSpec((4, 2, 4, 32, nodes), lambda p: (0, p, 0, 0, 0)),
        ],
        out_specs=pl.BlockSpec((16, 1, 32, 384), lambda p: (0, p, 0, 0)),
        out_shape=jax.ShapeDtypeStruct((16, 2, 32, 384), jnp.bfloat16),
        scratch_shapes=[pltpu.VMEM((2, 192, nodes), jnp.bfloat16)],
        compiler_params=params(),
    )(zh, y, leg)


def solve_kernel(coeffs_ref, known_ref, inverse_ref, out_ref, side, solved):
    nr = known_ref.shape[-1]
    lanes = matches(lambda i: ((i // 32) % 4) * 128 + (i // 128) * 32 + i % 32, (512, 512))
    swap = matches(lambda i: (i % 16) * 16 + i // 16, (256, 256))
    grouped = []
    for g in range(3):
        wide = jnp.concatenate(
            [coeffs_ref[x, :, :, g * LANES : (g + 1) * LANES].reshape(256, LANES) for x in range(4)], axis=1
        )
        grouped.append(jnp.dot(wide, lanes, preferred_element_type=jnp.float32).astype(jnp.bfloat16))
    for cf in range(6):
        rights = []
        for kk in range(2):
            q = kk * 6 + cf
            coeffs = grouped[q // 4][:, (q % 4) * nr : (q % 4 + 1) * nr].astype(jnp.float32)
            known = known_ref[:, kk, cf].reshape(256, nr).astype(jnp.float32)
            rights.append((known + section_step * coeffs).astype(jnp.bfloat16).reshape(8, 32, nr))
        for h in range(2):
            both = jnp.concatenate([right[:, h * 16 : (h + 1) * 16] for right in rights], axis=0)
            side[h * 16 : (h + 1) * 16, cf * 16 : (cf + 1) * 16] = moved_rows(
                swap, both.reshape(256, nr)
            ).reshape(16, 16, nr)
    for k in range(32):
        solved[k] = lax.dot_general(
            side[k], inverse_ref[k], (((1,), (1,)), ((), ())), preferred_element_type=jnp.float32
        ).astype(jnp.bfloat16)
    for cf in range(6):
        for h in range(2):
            here = solved[h * 16 : (h + 1) * 16, cf * 16 : (cf + 1) * 16]
            back = moved_rows(swap, here.reshape(256, nr)).reshape(2, 8, 16, nr)
            for kk in range(2):
                out_ref[:, kk, cf, h * 16 : (h + 1) * 16] = back[kk]


def radial_solve(coeffs, known, inverse):
    nr = known.shape[-1]
    return pl.pallas_call(
        solve_kernel,
        out_shape=jax.ShapeDtypeStruct(known.shape, jnp.bfloat16),
        scratch_shapes=[pltpu.VMEM((32, 96, nr), jnp.bfloat16)] * 2,
        compiler_params=params(),
    )(coeffs, known, inverse)


def legendre_by_slot(legendre, zh):
    pieces = []
    for d in range(4):
        piece = lax.dynamic_slice_in_dim(legendre, ((zh + d) & 3) * 4, 4, axis=0)
        if d:
            piece = lax.ppermute(piece, "zh", [(i, (i + d) % 4) for i in range(4)])
        pieces.append(piece)
    return pieces


def body(velocity, vorticity, m_of_slot, legendre, known_term, inverse):
    zh = lax.axis_index("zh")
    table = phase_rows(m_of_slot, velocity.shape[2] * 32, 4, 4)
    pieces = legendre_by_slot(legendre, zh)
    table, *pieces = lax.optimization_barrier((table, *pieces))
    leg = jnp.stack(pieces, axis=1)
    blocks = lamb_blocks(velocity, vorticity)
    blocks = lax.all_to_all(blocks, "long", split_axis=0, concat_axis=0, tiled=True)
    blocks, leg = lax.optimization_barrier((blocks, leg))
    leg = lax.all_gather(leg, "x", axis=0, tiled=False)
    fourier = dft(blocks, table)
    fourier = fourier.reshape(-1, 8, 3 * LANES)
    fourier = lax.all_to_all(fourier, ("zh", "long"), split_axis=0, concat_axis=0, tiled=True)
    coeffs = legendre_step(zh.reshape(1), fourier.reshape(-1, 3 * LANES), leg)
    coeffs = lax.all_to_all(coeffs, ("x", "zh"), split_axis=0, concat_axis=0, tiled=True)
    nr = known_term.shape[-1]
    solved = radial_solve(
        coeffs.reshape(4, 8, 32, 384), known_term.reshape(8, 2, 6, 32, nr), inverse
    )
    return solved.reshape(known_term.shape)


def solution(mesh):
    mesh = Mesh(mesh.devices.reshape(4, 4, 32), ("x", "zh", "long"))
    wide = ("x", "zh")
    return jax.shard_map(
        body,
        mesh=mesh,
        in_specs=(
            P(None, wide, "long", None),
            P(None, wide, "long", None),
            P(),
            P("long", wide, None),
            P("long", None, None, wide, None),
            P(wide, None, None),
        ),
        out_specs=P("long", None, None, wide, None),
        check_vma=False,
    )
```

time: 193 us -> 194 us (level)
  blocking collectives: 105 us -> 52 us
  starting transfers between devices: 23.3 us -> 42.7 us
  waiting for transfers between devices: 31.2 us -> 49.8 us
  between operations: 0.11 us -> 13.6 us
    all_to_all x2 -> x1, blocking collectives: 105 us -> 52 us  [body(): lax.all_to_all(coeffs, ('x', 'zh'), split_axis=0, concat_axis=0, tiled=True)]
    ppermute x0 -> x3, starting transfers between devices: none -> 22.5 us  [legendre_by_slot(): piece = lax.ppermute(piece, 'zh', [(i, (i + d) % 4) for i in range(4)])]
    all_gather x0 -> x1, waiting for transfers between devices: none -> 20.9 us  [body(): leg = lax.all_gather(leg, 'x', axis=0, tiled=False)]
    all_to_all x1, waiting for transfers between devices: 28.9 us -> 21.5 us  [body(): lax.all_to_all(fourier, ('zh', 'long'), split_axis=0, concat_axis=0, tile...]
    ppermute x0 -> x3, waiting for transfers between devices: none -> 7.33 us  [legendre_by_slot(): piece = lax.ppermute(piece, 'zh', [(i, (i + d) % 4) for i in range(4)])]
    all_to_all x1, starting transfers between devices: 16.8 us -> 11.1 us  [body(): lax.all_to_all(fourier, ('zh', 'long'), split_axis=0, concat_axis=0, tile...]
    all_to_all x1, starting transfers between devices: 6.52 us -> 9.09 us  [body(): lax.all_to_all(blocks, 'long', split_axis=0, concat_axis=0, tiled=True)]
    reshape x4 -> x2, local copies, waits for them, and re-layouts: 2.61 us -> 0.23 us  [phase_rows(): modes = m_of_slot.reshape(-1, groups, subs).transpose(1, 0, 2).reshape(-1)]
  transfers between devices with their start and end apart: 2 -> 6, of which waited for: 2 -> 3; matrix products, arithmetic and copies ran while one was open for 9% -> 11% of each run, Pallas kernels for 2% -> 1%
where the time goes in v2:
time: 194 us; the launch traced here: 193 us
  blocking collectives  52 us (27%)
  waiting for transfers between devices  49.8 us (26%)
  starting transfers between devices  42.7 us (22%)
  other arithmetic  19.4 us (10%)
  between operations  13.6 us (7%)
  Pallas kernels  10.3 us (5%)
  local copies, waits for them, and re-layouts  5.47 us (3%)
    all_to_all x1, blocking collectives, body(): lax.all_to_all(coeffs, ('x', 'zh'), split_axis=0, concat_axis=0, tiled=True)  52 us
    ppermute x3, starting transfers between devices, legendre_by_slot(): piece = lax.ppermute(piece, 'zh', [(i, (i + d) % 4) for i in range(4)])  22.5 us
    all_to_all x1, waiting for transfers between devices, body(): lax.all_to_all(fourier, ('zh', 'long'), split_axis=0, concat_axis=0, tile...  21.5 us
    all_gather x1, waiting for transfers between devices, body(): leg = lax.all_gather(leg, 'x', axis=0, tiled=False)  20.9 us
    convert_element_type x1, other arithmetic, phase_rows(): return (math.sqrt(2.0 / points) * jnp.cos(angle)).astype(jnp.bfloat16)  17.6 us
    all_to_all x1, starting transfers between devices, body(): lax.all_to_all(fourier, ('zh', 'long'), split_axis=0, concat_axis=0, tile...  11.1 us
    all_to_all x1, starting transfers between devices, body(): lax.all_to_all(blocks, 'long', split_axis=0, concat_axis=0, tiled=True)  9.09 us
    ppermute x3, waiting for transfers between devices, legendre_by_slot(): piece = lax.ppermute(piece, 'zh', [(i, (i + d) % 4) for i in range(4)])  7.33 us
  transfers between devices with their start and end apart: 6, of which 3 were waited for; matrix products, arithmetic and copies ran while one was open for 11% of the time, Pallas kernels for 1%

profile of v2, /device:TPU:32, one launch (start us, length us, event | category | flops | bytes accessed | tf_op | source)
XLA Modules:
  0.0 193.4 jit_solution(15090041610824147614)
XLA Ops:
  6.5 1.1 copy-done.2
  7.7 1.1 copy-done.3
  8.8 2.9 %shard_map.64 = bf16[32,3,32,128]{3,2,1,0:T(8,128)(2,1)} custom-call(bf16[3,8,32,512]{3,2,1,0:T(8,128)(2,1)S(1)} %copy-done.2, bf16[3,8,32,512]{3,2,1,0:T(8,128)(2,1)S(1)} %copy-done.3), custom_call_target="tpu_custom_call" | custom-call | tf_op jit(solution)/shard_map/pallas_call | solution.py:34
  11.7 9.1 %all-to-all-start = ((bf16[32,3,32,128]{3,2,1,0:T(8,128)(2,1)}), bf16[32,3,32,128]{3,2,1,0:T(8,128)(2,1)S(1)}, u32[]{:S(2)}, u32[]{:S(2)}) async-start(bf16[32,3,32,128]{3,2,1,0:T(8,128)(2,1)} %shard_map.64), calls=%async_computation | async-start | bytes 1572864 | tf_op jit(solution)/shard_map/all_to_all | solution.py:199
  20.8 0.0 all-gather.3.cloned.1.call-start
  20.9 0.0 copy-done.5
  21.0 9.7 %collective-permute-start.2 = (bf16[4,32,512]{2,1,0:T(8,128)(2,1)S(1)}, bf16[4,32,512]{2,1,0:T(8,128)(2,1)S(1)}, u32[]{:S(2)}, u32[]{:S(2)}) collective-permute-start(bf16[4,32,512]{2,1,0:T(8,128)(2,1)S(1)} %get-tuple-element.19), channel_id=1, source_target_pairs={{0,96},{32,0},{64,32},{96,64},{1,97},{33,1},{65,33},{97,65},{2,98}... | collective-permute-start | bytes 393224 | tf_op jit(solution)/shard_map/ppermute | solution.py:187
  30.7 1.9 collective-permute-start
  32.6 10.8 %collective-permute-start.1 = (bf16[4,32,512]{2,1,0:T(8,128)(2,1)S(1)}, bf16[4,32,512]{2,1,0:T(8,128)(2,1)}, u32[]{:S(2)}, u32[]{:S(2)}) collective-permute-start(bf16[4,32,512]{2,1,0:T(8,128)(2,1)S(1)} %get-tuple-element.22), channel_id=1, source_target_pairs={{0,64},{32,96},{64,0},{96,32},{1,65},{33,97},{65,1},{97,33},{2,66}... | collective-permute-start | bytes 393224 | tf_op jit(solution)/shard_map/ppermute | solution.py:187
  43.5 0.0 copy-done.6
  43.5 0.1 reshape.37
  43.6 0.1 reshape.38
  43.7 0.1 broadcast_in_dim.2
  43.9 0.2 mul.50
  44.0 17.6 %fusion.5.table_ref = bf16[1024,1024]{1,0:T(8,128)(2,1)S(1)} fusion(s32[1024]{0:T(1024)S(1)} %fusion.6, s32[1024]{0:T(1024)S(1)} %mul.50), kind=kLoop, calls=%fused_computation.8 | loop fusion | flops 17825792 | bytes 2105344 | tf_op jit(solution)/shard_map/convert_element_type | solution.py:51
  61.6 0.0 collective-permute-done.2
  61.6 7.3 %collective-permute-done = bf16[4,32,512]{2,1,0:T(8,128)(2,1)} collective-permute-done((bf16[4,32,512]{2,1,0:T(8,128)(2,1)S(1)}, bf16[4,32,512]{2,1,0:T(8,128)(2,1)}, u32[]{:S(2)}, u32[]{:S(2)}) %collective-permute-start) | collective-permute-done | bytes 131104 | tf_op jit(solution)/shard_map/ppermute | solution.py:187
  69.0 0.0 collective-permute-done.1
  69.0 1.9 pad_maximum_fusion
  70.8 0.0 all-to-all-done.x_ref
  70.8 0.0 all-gather.3.cloned.1.call-update
  70.9 1.7 shard_map.65
  72.6 0.0 copy-start
  72.6 0.9 copy-done
  73.5 11.1 %all-to-all-start.1 = ((bf16[128,8,384]{2,1,0:T(8,128)(2,1)}), bf16[128,8,384]{2,1,0:T(8,128)(2,1)S(1)}, u32[]{:S(2)}, u32[]{:S(2)}) async-start(bf16[128,8,384]{2,1,0:T(8,128)(2,1)} %bitcast.13), calls=%async_computation.1 | async-start | bytes 1572864 | tf_op jit(solution)/shard_map/all_to_all | solution.py:204
  84.6 20.9 %all-gather.3.cloned.1.call-done = bf16[16,4,32,512]{3,2,0,1:T(8,128)(2,1)} async-done(((bf16[4,4,32,512]{3,2,0,1:T(8,128)(2,1)}), bf16[16,4,32,512]{3,2,0,1:T(8,128)(2,1)}) %all-gather.3.cloned.1.call-update) | async-done | bytes 2097168 | tf_op jit(solution)/shard_map/all_gather | solution.py:201
  105.6 1.7 copy.9
  107.3 21.5 %all-to-all-done.1 = bf16[128,8,384]{2,1,0:T(8,128)(2,1)S(1)} async-done(((bf16[128,8,384]{2,1,0:T(8,128)(2,1)}), bf16[128,8,384]{2,1,0:T(8,128)(2,1)S(1)}, u32[]{:S(2)}, u32[]{:S(2)}) %all-to-all-start.1) | async-done | bytes 786464 | tf_op jit(solution)/shard_map/all_to_all | solution.py:204
  128.8 2.4 %shard_map.66 = bf16[16,2,32,384]{3,2,1,0:T(8,128)(2,1)S(1)} custom-call(s32[1]{0:T(128)} %bitcast.zh_ref, bf16[1024,384]{1,0:T(8,128)(2,1)S(1)} %bitcast.14, bf16[4,4,4,32,512]{4,3,2,1,0:T(8,128)(2,1)S(1)} %bitcast.12), custom_call_target="tpu_custom_call" | custom-call | tf_op jit(solution)/shard_map/pallas_call | solution.py:123
  131.3 52.0 %all_to_all.15 = bf16[16,2,32,384]{3,2,1,0:T(8,128)(2,1)S(1)} all-to-all(bf16[16,2,32,384]{3,2,1,0:T(8,128)(2,1)S(1)} %shard_map.66), channel_id=1, replica_groups=mesh['x'=4,'zh'=4,'long'=32] {'x','zh'}, dimensions={0} | all-to-all | bytes 1572864 | tf_op jit(solution)/shard_map/all_to_all | solution.py:206
  183.3 0.0 copy-done.4
  183.3 3.2 %shard_map.67 = bf16[8,2,6,32,128]{4,3,2,1,0:T(8,128)(2,1)} custom-call(bf16[4,8,32,384]{3,2,1,0:T(8,128)(2,1)S(1)} %bitcast.15, bf16[8,2,6,32,128]{4,3,2,1,0:T(8,128)(2,1)S(1)} %bitcast.16, bf16[32,128,128]{2,1,0:T(8,128)(2,1)S(1)} %copy-done.1), custom_call_target="tpu_custom_call" | custom-call | tf_op jit(solution)/shard_map/pallas_call | solution.py:174
  (10 shorter events, 0.1 us)
Async XLA Ops:
  6.5 1.1 copy-start.2
  7.7 1.1 copy-start.3
  8.8 12.1 %copy-start.5 = (bf16[16,32,512]{2,1,0:T(8,128)(2,1)S(1)}, bf16[16,32,512]{2,1,0:T(8,128)(2,1)}, u32[]{:S(2)}) copy-start(bf16[16,32,512]{2,1,0:T(8,128)(2,1)} %param.9) | copy-start | bytes 1572868
  8.8 34.7 %copy-start.6 = (s32[512]{0:T(512)S(1)}, s32[512]{0:T(512)}, u32[]{:S(2)}) copy-start(s32[512]{0:T(512)} %param.8) | copy-start | bytes 6148
  11.7 59.1 %all-to-all-start = ((bf16[32,3,32,128]{3,2,1,0:T(8,128)(2,1)}), bf16[32,3,32,128]{3,2,1,0:T(8,128)(2,1)S(1)}, u32[]{:S(2)}, u32[]{:S(2)}) async-start(bf16[32,3,32,128]{3,2,1,0:T(8,128)(2,1)} %shard_map.64), calls=%async_computation | async-start | bytes 1572864 | tf_op jit(solution)/shard_map/all_to_all | solution.py:199
  20.8 84.7 %all-gather.3.cloned.1.call-start = ((), (), s32[]{:S(2)}) async-start(), calls=%async_computation.3 | async-start | bytes 2621440 | tf_op jit(solution)/shard_map/all_gather | solution.py:201
  21.0 40.7 %collective-permute-start.2 = (bf16[4,32,512]{2,1,0:T(8,128)(2,1)S(1)}, bf16[4,32,512]{2,1,0:T(8,128)(2,1)S(1)}, u32[]{:S(2)}, u32[]{:S(2)}) collective-permute-start(bf16[4,32,512]{2,1,0:T(8,128)(2,1)S(1)} %get-tuple-element.19), channel_id=1, source_target_pairs={{0,96},{32,0},{64,32},{96,64},{1,97},{33,1},{65,33},{97,65},{2,98}... | collective-permute-start | bytes 393224 | tf_op jit(solution)/shard_map/ppermute | solution.py:187
  30.7 38.3 %collective-permute-start = (bf16[4,32,512]{2,1,0:T(8,128)(2,1)S(1)}, bf16[4,32,512]{2,1,0:T(8,128)(2,1)}, u32[]{:S(2)}, u32[]{:S(2)}) collective-permute-start(bf16[4,32,512]{2,1,0:T(8,128)(2,1)S(1)} %get-tuple-element.20), channel_id=1, source_target_pairs={{0,32},{32,64},{64,96},{96,0},{1,33},{33,65},{65,97},{97,1},{2,34}... | collective-permute-start | bytes 393224 | tf_op jit(solution)/shard_map/ppermute | solution.py:187
  32.6 36.3 %collective-permute-start.1 = (bf16[4,32,512]{2,1,0:T(8,128)(2,1)S(1)}, bf16[4,32,512]{2,1,0:T(8,128)(2,1)}, u32[]{:S(2)}, u32[]{:S(2)}) collective-permute-start(bf16[4,32,512]{2,1,0:T(8,128)(2,1)S(1)} %get-tuple-element.22), channel_id=1, source_target_pairs={{0,64},{32,96},{64,0},{96,32},{1,65},{33,97},{65,1},{97,33},{2,66}... | collective-permute-start | bytes 393224 | tf_op jit(solution)/shard_map/ppermute | solution.py:187
  72.6 0.9 copy-start
  73.5 55.4 %all-to-all-start.1 = ((bf16[128,8,384]{2,1,0:T(8,128)(2,1)}), bf16[128,8,384]{2,1,0:T(8,128)(2,1)S(1)}, u32[]{:S(2)}, u32[]{:S(2)}) async-start(bf16[128,8,384]{2,1,0:T(8,128)(2,1)} %bitcast.13), calls=%async_computation.1 | async-start | bytes 1572864 | tf_op jit(solution)/shard_map/all_to_all | solution.py:204
  128.8 54.5 %copy-start.1 = (bf16[32,128,128]{2,1,0:T(8,128)(2,1)S(1)}, bf16[32,128,128]{2,1,0:T(8,128)(2,1)}, u32[]{:S(2)}) copy-start(bf16[32,128,128]{2,1,0:T(8,128)(2,1)} %inverse_ref.1) | copy-start | bytes 3145732
  128.8 54.5 %copy-start.4 = (bf16[16,2,3,32,128]{4,3,2,1,0:T(8,128)(2,1)S(1)}, bf16[16,2,3,32,128]{4,3,2,1,0:T(8,128)(2,1)}, u32[]{:S(2)}) copy-start(bf16[16,2,3,32,128]{4,3,2,1,0:T(8,128)(2,1)} %param.10) | copy-start | bytes 2359300
Sparse Core Ops, SparseCore 0:
  71.0 34.5 all-gather.2

commit v3 on v2

--- a/solution.py
+++ b/solution.py
@@ -13,8 +13,8 @@
 LANES = 128
 
 
-def params():
-    return pltpu.CompilerParams(vmem_limit_bytes=VMEM_LIMIT)
+def params(limit=VMEM_LIMIT):
+    return pltpu.CompilerParams(vmem_limit_bytes=limit)
 
 
 def lamb_kernel(vel_ref, vort_ref, out_ref):
@@ -37,7 +37,7 @@
         in_specs=[spec, spec],
         out_specs=pl.BlockSpec((tbs, 3, nj, LANES), lambda r: (r, 0, 0, 0)),
         out_shape=jax.ShapeDtypeStruct((nr * tbs, 3, nj, LANES), jnp.bfloat16),
-        compiler_params=params(),
+        compiler_params=params(60 * 1024 * 1024),
     )(velocity, vorticity)
 
 
@@ -83,8 +83,8 @@
     return jnp.dot(matrix, array, preferred_element_type=jnp.float32).astype(jnp.bfloat16)
 
 
-def legendre_kernel(zh_ref, y_ref, leg_ref, out_ref, side):
-    zh = zh_ref[0]
+def legendre_kernel(place_ref, y_ref, leg0_ref, leg1_ref, leg2_ref, leg3_ref, out_ref, side):
+    place_x, zh = place_ref[0], place_ref[1]
     pair = pl.program_id(0)
     for kk in range(2):
         k = pair * 2 + kk
@@ -103,10 +103,10 @@
                         side[kk, start : start + 16, tb * LANES : (tb + 1) * LANES] = moved[
                             (tb * 2 + c) * 16 : (tb * 2 + c) * 16 + 16, f * LANES : (f + 1) * LANES
                         ]
-    for x in range(4):
+    for e, leg_ref in enumerate((leg0_ref, leg1_ref, leg2_ref, leg3_ref)):
         coeffs = [
             lax.dot_general(
-                leg_ref[x, kk].reshape(128, -1),
+                leg_ref[:, kk].reshape(128, -1),
                 side[kk],
                 (((1,), (1,)), ((), ())),
                 preferred_element_type=jnp.float32,
@@ -115,24 +115,24 @@
         ]
         both = jnp.concatenate(coeffs, axis=1)
         for d in range(4):
-            out_ref[x * 4 + ((zh - d) & 3), 0] = both[d * 32 : (d + 1) * 32, :]
-
-
-def legendre_step(zh, y, leg):
-    nodes = leg.shape[-1]
+            out_ref[((place_x - e) & 3) * 4 + ((zh - d) & 3), 0] = both[d * 32 : (d + 1) * 32, :]
+
+
+def legendre_step(place, y, legs):
+    nodes = legs[0].shape[-1]
     return pl.pallas_call(
         legendre_kernel,
         grid=(2,),
         in_specs=[
             pl.BlockSpec(memory_space=pltpu.SMEM),
             pl.BlockSpec(y.shape, lambda p: (0, 0)),
-            pl.BlockSpec((4, 2, 4, 32, nodes), lambda p: (0, p, 0, 0, 0)),
-        ],
+        ]
+        + [pl.BlockSpec((4, 2, 32, nodes), lambda p: (0, p, 0, 0))] * 4,
         out_specs=pl.BlockSpec((16, 1, 32, 384), lambda p: (0, p, 0, 0)),
         out_shape=jax.ShapeDtypeStruct((16, 2, 32, 384), jnp.bfloat16),
         scratch_shapes=[pltpu.VMEM((2, 192, nodes), jnp.bfloat16)],
         compiler_params=params(),
-    )(zh, y, leg)
+    )(place, y, *legs)
 
 
 def solve_kernel(coeffs_ref, known_ref, inverse_ref, out_ref, side, solved):
@@ -190,19 +190,19 @@
 
 
 def body(velocity, vorticity, m_of_slot, legendre, known_term, inverse):
-    zh = lax.axis_index("zh")
+    place_x, zh = lax.axis_index("x"), lax.axis_index("zh")
     table = phase_rows(m_of_slot, velocity.shape[2] * 32, 4, 4)
     pieces = legendre_by_slot(legendre, zh)
     table, *pieces = lax.optimization_barrier((table, *pieces))
-    leg = jnp.stack(pieces, axis=1)
     blocks = lamb_blocks(velocity, vorticity)
     blocks = lax.all_to_all(blocks, "long", split_axis=0, concat_axis=0, tiled=True)
-    blocks, leg = lax.optimization_barrier((blocks, leg))
-    leg = lax.all_gather(leg, "x", axis=0, tiled=False)
+    blocks, *pieces = lax.optimization_barrier((blocks, *pieces))
+    leg = jnp.stack(pieces, axis=0)
+    legs = [leg] + [lax.ppermute(leg, "x", [(i, (i + e) % 4) for i in range(4)]) for e in (1, 2, 3)]
     fourier = dft(blocks, table)
     fourier = fourier.reshape(-1, 8, 3 * LANES)
     fourier = lax.all_to_all(fourier, ("zh", "long"), split_axis=0, concat_axis=0, tiled=True)
-    coeffs = legendre_step(zh.reshape(1), fourier.reshape(-1, 3 * LANES), leg)
+    coeffs = legendre_step(jnp.stack([place_x, zh]), fourier.reshape(-1, 3 * LANES), legs)
     coeffs = lax.all_to_all(coeffs, ("x", "zh"), split_axis=0, concat_axis=0, tiled=True)
     nr = known_term.shape[-1]
     solved = radial_solve(

time: 194 us -> 181 us (0.933)
  between operations: 13.6 us -> 0.19 us
  starting transfers between devices: 42.7 us -> 52.9 us
  waiting for transfers between devices: 49.8 us -> 39.7 us
  Pallas kernels: 10.3 us -> 13.4 us
    ppermute x0 -> x3, waiting for transfers between devices: none -> 22.7 us  [body(): lax.ppermute(leg, 'x', [(i, (i + e) % 4) for i in range(4)])]
    all_gather x1 -> x0, waiting for transfers between devices: 20.9 us -> none  [body(): leg = lax.all_gather(leg, 'x', axis=0, tiled=False)]
    all_to_all x1, waiting for transfers between devices: 21.5 us -> 10.3 us  [body(): lax.all_to_all(fourier, ('zh', 'long'), split_axis=0, concat_axis=0, tile...]
    ppermute x0 -> x3, starting transfers between devices: none -> 10.2 us  [body(): lax.ppermute(leg, 'x', [(i, (i + e) % 4) for i in range(4)])]
    pallas_call x1, Pallas kernels: 2.92 us -> 5.49 us  [lamb_blocks(): pl.pallas_call(lamb_kernel, grid=(nr,), in_specs=[spec, spec], out_specs=...]
  transfers between devices with their start and end apart: 6 -> 8, of which waited for: 3 -> 4; matrix products, arithmetic and copies ran while one was open for 11% -> 11% of each run, Pallas kernels for 1% -> 0%
where the time goes in v3:
time: 181 us; the launch traced here: 180 us
  starting transfers between devices  52.9 us (29%)
  blocking collectives  52 us (29%)
  waiting for transfers between devices  39.7 us (22%)
  other arithmetic  17.7 us (10%)
  Pallas kernels  13.4 us (7%)
  local copies, waits for them, and re-layouts  4 us (2%)
    all_to_all x1, blocking collectives, body(): lax.all_to_all(coeffs, ('x', 'zh'), split_axis=0, concat_axis=0, tiled=True)  52 us
    ppermute x3, waiting for transfers between devices, body(): lax.ppermute(leg, 'x', [(i, (i + e) % 4) for i in range(4)])  22.7 us
    ppermute x3, starting transfers between devices, legendre_by_slot(): piece = lax.ppermute(piece, 'zh', [(i, (i + d) % 4) for i in range(4)])  22.5 us
    convert_element_type x1, other arithmetic, phase_rows(): return (math.sqrt(2.0 / points) * jnp.cos(angle)).astype(jnp.bfloat16)  17.6 us
    all_to_all x1, starting transfers between devices, body(): lax.all_to_all(fourier, ('zh', 'long'), split_axis=0, concat_axis=0, tile...  11.2 us
    all_to_all x1, waiting for transfers between devices, body(): lax.all_to_all(fourier, ('zh', 'long'), split_axis=0, concat_axis=0, tile...  10.3 us
    ppermute x3, starting transfers between devices, body(): lax.ppermute(leg, 'x', [(i, (i + e) % 4) for i in range(4)])  10.2 us
    all_to_all x1, starting transfers between devices, body(): lax.all_to_all(blocks, 'long', split_axis=0, concat_axis=0, tiled=True)  9.09 us
  transfers between devices with their start and end apart: 8, of which 4 were waited for; matrix products, arithmetic and copies ran while one was open for 11% of the time, Pallas kernels for 0%

profile of v3, /device:TPU:32, one launch (start us, length us, event | category | flops | bytes accessed | tf_op | source)
XLA Modules:
  0.0 180.0 jit_solution(9332437042218004252)
XLA Ops:
  0.0 5.5 %shard_map.64 = bf16[32,3,32,128]{3,2,1,0:T(8,128)(2,1)} custom-call(bf16[3,8,32,512]{3,2,1,0:T(8,128)(2,1)} %vel_ref.1, bf16[3,8,32,512]{3,2,1,0:T(8,128)(2,1)} %vort_ref.1), custom_call_target="tpu_custom_call" | custom-call | tf_op jit(solution)/shard_map/pallas_call | solution.py:34
  5.5 9.1 %all-to-all-start = ((bf16[32,3,32,128]{3,2,1,0:T(8,128)(2,1)}), bf16[32,3,32,128]{3,2,1,0:T(8,128)(2,1)S(1)}, u32[]{:S(2)}, u32[]{:S(2)}) async-start(bf16[32,3,32,128]{3,2,1,0:T(8,128)(2,1)} %shard_map.64), calls=%async_computation | async-start | bytes 1572864 | tf_op jit(solution)/shard_map/all_to_all | solution.py:198
  14.6 0.7 constant_dynamic-slice_fusion
  15.4 9.7 %collective-permute-start.2 = (bf16[4,32,512]{2,1,0:T(8,128)(2,1)}, bf16[4,32,512]{2,1,0:T(8,128)(2,1)S(1)}, u32[]{:S(2)}, u32[]{:S(2)}) collective-permute-start(bf16[4,32,512]{2,1,0:T(8,128)(2,1)} %get-tuple-element.25), channel_id=1, source_target_pairs={{0,96},{32,0},{64,32},{96,64},{1,97},{33,1},{65,33},{97,65},{2,98}... | collective-permute-start | bytes 393224 | tf_op jit(solution)/shard_map/ppermute | solution.py:187
  25.1 1.9 %collective-permute-start = (bf16[4,32,512]{2,1,0:T(8,128)(2,1)}, bf16[4,32,512]{2,1,0:T(8,128)(2,1)S(1)}, u32[]{:S(2)}, u32[]{:S(2)}) collective-permute-start(bf16[4,32,512]{2,1,0:T(8,128)(2,1)} %get-tuple-element.26), channel_id=1, source_target_pairs={{0,32},{32,64},{64,96},{96,0},{1,33},{33,65},{65,97},{97,1},{2,34}... | collective-permute-start | bytes 393224 | tf_op jit(solution)/shard_map/ppermute | solution.py:187
  27.0 10.8 %collective-permute-start.1 = (bf16[4,32,512]{2,1,0:T(8,128)(2,1)S(1)}, bf16[4,32,512]{2,1,0:T(8,128)(2,1)S(1)}, u32[]{:S(2)}, u32[]{:S(2)}) collective-permute-start(bf16[4,32,512]{2,1,0:T(8,128)(2,1)S(1)} %get-tuple-element.28), channel_id=1, source_target_pairs={{0,64},{32,96},{64,0},{96,32},{1,65},{33,97},{65,1},{97,33},{2,66}... | collective-permute-start | bytes 393224 | tf_op jit(solution)/shard_map/ppermute | solution.py:187
  37.9 0.1 reshape.33
  38.0 0.1 reshape.34
  38.1 0.1 broadcast_in_dim.2
  38.3 0.2 mul.50
  38.4 17.6 %fusion.5.table_ref = bf16[1024,1024]{1,0:T(8,128)(2,1)S(1)} fusion(s32[1024]{0:T(1024)S(1)} %fusion.6, s32[1024]{0:T(1024)S(1)} %mul.50), kind=kLoop, calls=%fused_computation.8 | loop fusion | flops 17825792 | bytes 2105344 | tf_op jit(solution)/shard_map/convert_element_type | solution.py:51
  56.0 0.0 collective-permute-done.2
  56.0 6.6 %collective-permute-done = bf16[4,32,512]{2,1,0:T(8,128)(2,1)S(1)} collective-permute-done((bf16[4,32,512]{2,1,0:T(8,128)(2,1)}, bf16[4,32,512]{2,1,0:T(8,128)(2,1)S(1)}, u32[]{:S(2)}, u32[]{:S(2)}) %collective-permute-start) | collective-permute-done | bytes 131104 | tf_op jit(solution)/shard_map/ppermute | solution.py:187
  62.7 0.0 collective-permute-done.1
  62.7 0.0 all-to-all-done.x_ref
  62.7 1.7 shard_map.65
  64.4 0.0 copy-start
  64.4 0.9 copy-done
  65.3 11.2 %all-to-all-start.1 = ((bf16[128,8,384]{2,1,0:T(8,128)(2,1)}), bf16[128,8,384]{2,1,0:T(8,128)(2,1)S(1)}, u32[]{:S(2)}, u32[]{:S(2)}) async-start(bf16[128,8,384]{2,1,0:T(8,128)(2,1)} %bitcast.12), calls=%async_computation.1 | async-start | bytes 1572864 | tf_op jit(solution)/shard_map/all_to_all | solution.py:204
  76.5 0.1 pad_maximum_fusion.leg0_ref
  76.6 4.7 %collective-permute-start.5 = (bf16[4,4,32,512]{3,2,1,0:T(8,128)(2,1)S(1)}, bf16[4,4,32,512]{3,2,1,0:T(8,128)(2,1)S(1)}, u32[]{:S(2)}, u32[]{:S(2)}) collective-permute-start(bf16[4,4,32,512]{3,2,1,0:T(8,128)(2,1)S(1)} %pad_maximum_fusion.leg0_ref), channel_id=1, source_target_pairs={{0,384},{128,0},{256,128},{384,256},{1,385},{129,1},{257,129},{385... | collective-permute-start | bytes 1572872 | tf_op jit(solution)/shard_map/ppermute | solution.py:201
  81.3 2.7 %collective-permute-start.4 = (bf16[4,4,32,512]{3,2,1,0:T(8,128)(2,1)S(1)}, bf16[4,4,32,512]{3,2,1,0:T(8,128)(2,1)S(1)}, u32[]{:S(2)}, u32[]{:S(2)}) collective-permute-start(bf16[4,4,32,512]{3,2,1,0:T(8,128)(2,1)S(1)} %pad_maximum_fusion.leg0_ref), channel_id=1, source_target_pairs={{0,256},{128,384},{256,0},{384,128},{1,257},{129,385},{257,1},{385... | collective-permute-start | bytes 1572872 | tf_op jit(solution)/shard_map/ppermute | solution.py:201
  84.0 2.8 %collective-permute-start.3 = (bf16[4,4,32,512]{3,2,1,0:T(8,128)(2,1)S(1)}, bf16[4,4,32,512]{3,2,1,0:T(8,128)(2,1)S(1)}, u32[]{:S(2)}, u32[]{:S(2)}) collective-permute-start(bf16[4,4,32,512]{3,2,1,0:T(8,128)(2,1)S(1)} %pad_maximum_fusion.leg0_ref), channel_id=1, source_target_pairs={{0,128},{128,256},{256,384},{384,0},{1,129},{129,257},{257,385},{3... | collective-permute-start | bytes 1572872 | tf_op jit(solution)/shard_map/ppermute | solution.py:201
  86.8 0.1 pad_add_fusion.place_ref
  86.9 17.1 %collective-permute-done.5.leg3_ref = bf16[4,4,32,512]{3,2,1,0:T(8,128)(2,1)S(1)} collective-permute-done((bf16[4,4,32,512]{3,2,1,0:T(8,128)(2,1)S(1)}, bf16[4,4,32,512]{3,2,1,0:T(8,128)(2,1)S(1)}, u32[]{:S(2)}, u32[]{:S(2)}) %collective-permute-start.5) | collective-permute-done | bytes 524320 | tf_op jit(solution)/shard_map/ppermute | solution.py:201
  104.0 5.6 %collective-permute-done.3.leg1_ref = bf16[4,4,32,512]{3,2,1,0:T(8,128)(2,1)S(1)} collective-permute-done((bf16[4,4,32,512]{3,2,1,0:T(8,128)(2,1)S(1)}, bf16[4,4,32,512]{3,2,1,0:T(8,128)(2,1)S(1)}, u32[]{:S(2)}, u32[]{:S(2)}) %collective-permute-start.3) | collective-permute-done | bytes 524320 | tf_op jit(solution)/shard_map/ppermute | solution.py:201
  109.6 0.8 copy-done.3
  110.4 10.3 %all-to-all-done.1 = bf16[128,8,384]{2,1,0:T(8,128)(2,1)S(1)} async-done(((bf16[128,8,384]{2,1,0:T(8,128)(2,1)}), bf16[128,8,384]{2,1,0:T(8,128)(2,1)S(1)}, u32[]{:S(2)}, u32[]{:S(2)}) %all-to-all-start.1) | async-done | bytes 786464 | tf_op jit(solution)/shard_map/all_to_all | solution.py:204
  120.7 1.0 copy-done.4
  121.8 2.9 %shard_map.66 = bf16[16,2,32,384]{3,2,1,0:T(8,128)(2,1)S(1)} custom-call(s32[2]{0:T(128)S(1)} %pad_add_fusion.place_ref, bf16[1024,384]{1,0:T(8,128)(2,1)S(1)} %bitcast.13, bf16[4,4,32,512]{3,2,1,0:T(8,128)(2,1)S(1)} %pad_maximum_fusion.leg0_ref, bf16[4,4,32,512]{3,2,1,0:T(8,128)(2,1)S(1)} %copy-done.4, ...), custom_call_target="tpu_custom_call" | custom-call | tf_op jit(solution)/shard_map/pallas_call | solution.py:123
  124.7 52.0 %all_to_all.15 = bf16[16,2,32,384]{3,2,1,0:T(8,128)(2,1)S(1)} all-to-all(bf16[16,2,32,384]{3,2,1,0:T(8,128)(2,1)S(1)} %shard_map.66), channel_id=1, replica_groups=mesh['x'=4,'zh'=4,'long'=32] {'x','zh'}, dimensions={0} | all-to-all | bytes 1572864 | tf_op jit(solution)/shard_map/all_to_all | solution.py:206
  176.8 3.2 %shard_map.67 = bf16[8,2,6,32,128]{4,3,2,1,0:T(8,128)(2,1)} custom-call(bf16[4,8,32,384]{3,2,1,0:T(8,128)(2,1)S(1)} %bitcast.14, bf16[8,2,6,32,128]{4,3,2,1,0:T(8,128)(2,1)S(1)} %bitcast.15, bf16[32,128,128]{2,1,0:T(8,128)(2,1)S(1)} %copy-done.1), custom_call_target="tpu_custom_call" | custom-call | tf_op jit(solution)/shard_map/pallas_call | solution.py:174
  (13 shorter events, 0.0 us)
Async XLA Ops:
  0.0 14.6 %copy-start.5 = (bf16[16,32,512]{2,1,0:T(8,128)(2,1)S(1)}, bf16[16,32,512]{2,1,0:T(8,128)(2,1)}, u32[]{:S(2)}) copy-start(bf16[16,32,512]{2,1,0:T(8,128)(2,1)} %param.9) | copy-start | bytes 1572868
  0.0 37.9 %copy-start.6 = (s32[512]{0:T(512)S(1)}, s32[512]{0:T(512)}, u32[]{:S(2)}) copy-start(s32[512]{0:T(512)} %param.8) | copy-start | bytes 6148
  5.5 57.2 %all-to-all-start = ((bf16[32,3,32,128]{3,2,1,0:T(8,128)(2,1)}), bf16[32,3,32,128]{3,2,1,0:T(8,128)(2,1)S(1)}, u32[]{:S(2)}, u32[]{:S(2)}) async-start(bf16[32,3,32,128]{3,2,1,0:T(8,128)(2,1)} %shard_map.64), calls=%async_computation | async-start | bytes 1572864 | tf_op jit(solution)/shard_map/all_to_all | solution.py:198
  15.4 40.7 %collective-permute-start.2 = (bf16[4,32,512]{2,1,0:T(8,128)(2,1)}, bf16[4,32,512]{2,1,0:T(8,128)(2,1)S(1)}, u32[]{:S(2)}, u32[]{:S(2)}) collective-permute-start(bf16[4,32,512]{2,1,0:T(8,128)(2,1)} %get-tuple-element.25), channel_id=1, source_target_pairs={{0,96},{32,0},{64,32},{96,64},{1,97},{33,1},{65,33},{97,65},{2,98}... | collective-permute-start | bytes 393224 | tf_op jit(solution)/shard_map/ppermute | solution.py:187
  25.1 37.6 %collective-permute-start = (bf16[4,32,512]{2,1,0:T(8,128)(2,1)}, bf16[4,32,512]{2,1,0:T(8,128)(2,1)S(1)}, u32[]{:S(2)}, u32[]{:S(2)}) collective-permute-start(bf16[4,32,512]{2,1,0:T(8,128)(2,1)} %get-tuple-element.26), channel_id=1, source_target_pairs={{0,32},{32,64},{64,96},{96,0},{1,33},{33,65},{65,97},{97,1},{2,34}... | collective-permute-start | bytes 393224 | tf_op jit(solution)/shard_map/ppermute | solution.py:187
  27.0 35.7 %collective-permute-start.1 = (bf16[4,32,512]{2,1,0:T(8,128)(2,1)S(1)}, bf16[4,32,512]{2,1,0:T(8,128)(2,1)S(1)}, u32[]{:S(2)}, u32[]{:S(2)}) collective-permute-start(bf16[4,32,512]{2,1,0:T(8,128)(2,1)S(1)} %get-tuple-element.28), channel_id=1, source_target_pairs={{0,64},{32,96},{64,0},{96,32},{1,65},{33,97},{65,1},{97,33},{2,66}... | collective-permute-start | bytes 393224 | tf_op jit(solution)/shard_map/ppermute | solution.py:187
  64.4 0.9 copy-start
  65.3 55.4 %all-to-all-start.1 = ((bf16[128,8,384]{2,1,0:T(8,128)(2,1)}), bf16[128,8,384]{2,1,0:T(8,128)(2,1)S(1)}, u32[]{:S(2)}, u32[]{:S(2)}) async-start(bf16[128,8,384]{2,1,0:T(8,128)(2,1)} %bitcast.12), calls=%async_computation.1 | async-start | bytes 1572864 | tf_op jit(solution)/shard_map/all_to_all | solution.py:204
  76.6 27.4 %collective-permute-start.5 = (bf16[4,4,32,512]{3,2,1,0:T(8,128)(2,1)S(1)}, bf16[4,4,32,512]{3,2,1,0:T(8,128)(2,1)S(1)}, u32[]{:S(2)}, u32[]{:S(2)}) collective-permute-start(bf16[4,4,32,512]{3,2,1,0:T(8,128)(2,1)S(1)} %pad_maximum_fusion.leg0_ref), channel_id=1, source_target_pairs={{0,384},{128,0},{256,128},{384,256},{1,385},{129,1},{257,129},{385... | collective-permute-start | bytes 1572872 | tf_op jit(solution)/shard_map/ppermute | solution.py:201
  81.3 22.7 %collective-permute-start.4 = (bf16[4,4,32,512]{3,2,1,0:T(8,128)(2,1)S(1)}, bf16[4,4,32,512]{3,2,1,0:T(8,128)(2,1)S(1)}, u32[]{:S(2)}, u32[]{:S(2)}) collective-permute-start(bf16[4,4,32,512]{3,2,1,0:T(8,128)(2,1)S(1)} %pad_maximum_fusion.leg0_ref), channel_id=1, source_target_pairs={{0,256},{128,384},{256,0},{384,128},{1,257},{129,385},{257,1},{385... | collective-permute-start | bytes 1572872 | tf_op jit(solution)/shard_map/ppermute | solution.py:201
  84.0 25.6 %collective-permute-start.3 = (bf16[4,4,32,512]{3,2,1,0:T(8,128)(2,1)S(1)}, bf16[4,4,32,512]{3,2,1,0:T(8,128)(2,1)S(1)}, u32[]{:S(2)}, u32[]{:S(2)}) collective-permute-start(bf16[4,4,32,512]{3,2,1,0:T(8,128)(2,1)S(1)} %pad_maximum_fusion.leg0_ref), channel_id=1, source_target_pairs={{0,128},{128,256},{256,384},{384,0},{1,129},{129,257},{257,385},{3... | collective-permute-start | bytes 1572872 | tf_op jit(solution)/shard_map/ppermute | solution.py:201
  109.6 0.8 copy-start.3
  120.7 1.0 copy-start.4
  121.8 55.0 %copy-start.1 = (bf16[32,128,128]{2,1,0:T(8,128)(2,1)S(1)}, bf16[32,128,128]{2,1,0:T(8,128)(2,1)}, u32[]{:S(2)}) copy-start(bf16[32,128,128]{2,1,0:T(8,128)(2,1)} %inverse_ref.1) | copy-start | bytes 3145732
  121.8 55.0 %copy-start.2 = (bf16[16,2,3,32,128]{4,3,2,1,0:T(8,128)(2,1)S(1)}, bf16[16,2,3,32,128]{4,3,2,1,0:T(8,128)(2,1)}, u32[]{:S(2)}) copy-start(bf16[16,2,3,32,128]{4,3,2,1,0:T(8,128)(2,1)} %param.10) | copy-start | bytes 2359300

commit v4 on v3

--- a/solution.py
+++ b/solution.py
@@ -10,6 +10,7 @@
 
 section_step = 0.75
 VMEM_LIMIT = 48 * 1024 * 1024
+LARGE = 60 * 1024 * 1024
 LANES = 128
 
 
@@ -18,37 +19,61 @@
 
 
 def lamb_kernel(vel_ref, vort_ref, out_ref):
-    vel = [vel_ref[i, 0].astype(jnp.float32) for i in range(3)]
-    vort = [vort_ref[i, 0].astype(jnp.float32) for i in range(3)]
-    for f in range(3):
-        a, b = (f + 1) % 3, (f + 2) % 3
-        lamb = (vel[a] * vort[b] - vel[b] * vort[a]).astype(jnp.bfloat16)
-        for tb in range(lamb.shape[1] // LANES):
-            out_ref[tb, f] = lamb[:, tb * LANES : (tb + 1) * LANES]
+    tbs = vel_ref.shape[3] // LANES
+    for r in range(vel_ref.shape[1]):
+        for tb in range(tbs):
+            lanes = slice(tb * LANES, (tb + 1) * LANES)
+            vel = [vel_ref[i, r, :, lanes].astype(jnp.float32) for i in range(3)]
+            vort = [vort_ref[i, r, :, lanes].astype(jnp.float32) for i in range(3)]
+            for f in range(3):
+                a, b = (f + 1) % 3, (f + 2) % 3
+                out_ref[r * tbs + tb, f] = (vel[a] * vort[b] - vel[b] * vort[a]).astype(jnp.bfloat16)
 
 
 def lamb_blocks(velocity, vorticity):
     _, nr, nj, nt = velocity.shape
     tbs = nt // LANES
-    spec = pl.BlockSpec((3, 1, nj, nt), lambda r: (0, r, 0, 0))
+    steps = 2
+    spec = pl.BlockSpec((3, nr // steps, nj, nt), lambda r: (0, r, 0, 0))
     return pl.pallas_call(
         lamb_kernel,
-        grid=(nr,),
+        grid=(steps,),
         in_specs=[spec, spec],
-        out_specs=pl.BlockSpec((tbs, 3, nj, LANES), lambda r: (r, 0, 0, 0)),
+        out_specs=pl.BlockSpec((nr // steps * tbs, 3, nj, LANES), lambda r: (r, 0, 0, 0)),
         out_shape=jax.ShapeDtypeStruct((nr * tbs, 3, nj, LANES), jnp.bfloat16),
-        compiler_params=params(60 * 1024 * 1024),
+        compiler_params=params(LARGE),
     )(velocity, vorticity)
+
+
+SINE = (6.283185160089461, -41.341655031412216, 81.6010040730263, -76.54978228858441, 39.53670603021233)
+
+
+def phase_kernel(mode_ref, out_ref):
+    rows, points = out_ref.shape
+    column = lax.broadcasted_iota(jnp.int32, (rows, points), 1).astype(jnp.float32)
+    parity = (lax.broadcasted_iota(jnp.int32, (rows, 1), 0) & 1).astype(jnp.float32)
+    turns = (mode_ref[...] * column + parity * (points / 4)) * (1.0 / points)
+    quarter = jnp.abs(turns - jnp.floor(turns) - 0.5) - 0.25
+    square = quarter * quarter
+    norm = math.sqrt(2.0 / points)
+    value = norm * SINE[4]
+    for power in (3, 2, 1, 0):
+        value = value * square + norm * SINE[power]
+    out_ref[...] = (value * quarter).astype(jnp.bfloat16)
 
 
 def phase_rows(m_of_slot, points, groups, subs):
     modes = m_of_slot.reshape(-1, groups, subs).transpose(1, 0, 2).reshape(-1)
-    paired = jnp.repeat(modes, 2)
-    parity = jnp.arange(paired.shape[0], dtype=jnp.int32) % 2
-    column = jnp.arange(points, dtype=jnp.int32)
-    product = (paired[:, None] * column[None, :] + parity[:, None] * (points // 4)) % points
-    angle = 2.0 * math.pi / points * product.astype(jnp.float32)
-    return (math.sqrt(2.0 / points) * jnp.cos(angle)).astype(jnp.bfloat16)
+    paired = jnp.repeat(modes, 2).astype(jnp.float32)[:, None]
+    rows, step = paired.shape[0], 256
+    return pl.pallas_call(
+        phase_kernel,
+        grid=(rows // step,),
+        in_specs=[pl.BlockSpec((step, 1), lambda i: (i, 0))],
+        out_specs=pl.BlockSpec((step, points), lambda i: (i, 0)),
+        out_shape=jax.ShapeDtypeStruct((rows, points), jnp.bfloat16),
+        compiler_params=params(),
+    )(paired)
 
 
 def dft_kernel(x_ref, table_ref, out_ref):

time: 181 us -> 178 us (0.983)
  other arithmetic: 17.7 us -> 1.18 us
  waiting for transfers between devices: 39.7 us -> 50.8 us
  Pallas kernels: 13.4 us -> 15.8 us
    convert_element_type x1, other arithmetic: 17.6 us -> 0.01 us  [phase_rows(): paired = jnp.repeat(modes, 2).astype(jnp.float32)[:, None]]
    ppermute x3, waiting for transfers between devices: 6.65 us -> 18.7 us  [legendre_by_slot(): piece = lax.ppermute(piece, 'zh', [(i, (i + d) % 4) for i in range(4)])]
    pallas_call x1 -> x2, Pallas kernels: 5.49 us -> 7.89 us  [the longest x1 5.58 us: phase_rows(): pl.pallas_call(phase_kernel, grid=(rows // step,), in_specs=[pl.BlockSpec...]
  transfers between devices with their start and end apart: 8 -> 8, of which waited for: 4 -> 4; matrix products, arithmetic and copies ran while one was open for 11% -> 1% of each run, Pallas kernels for 0% -> 3%
where the time goes in v4:
time: 178 us; the launch traced here: 177 us
  starting transfers between devices  52.9 us (30%)
  blocking collectives  52.1 us (29%)
  waiting for transfers between devices  50.8 us (29%)
  Pallas kernels  15.8 us (9%)
  local copies, waits for them, and re-layouts  4.02 us (2%)
    all_to_all x1, blocking collectives, body(): lax.all_to_all(coeffs, ('x', 'zh'), split_axis=0, concat_axis=0, tiled=True)  52.1 us
    ppermute x3, waiting for transfers between devices, body(): lax.ppermute(leg, 'x', [(i, (i + e) % 4) for i in range(4)])  22.7 us
    ppermute x3, starting transfers between devices, legendre_by_slot(): piece = lax.ppermute(piece, 'zh', [(i, (i + d) % 4) for i in range(4)])  22.5 us
    ppermute x3, waiting for transfers between devices, legendre_by_slot(): piece = lax.ppermute(piece, 'zh', [(i, (i + d) % 4) for i in range(4)])  18.7 us
    all_to_all x1, starting transfers between devices, body(): lax.all_to_all(fourier, ('zh', 'long'), split_axis=0, concat_axis=0, tile...  11.2 us
    ppermute x3, starting transfers between devices, body(): lax.ppermute(leg, 'x', [(i, (i + e) % 4) for i in range(4)])  10.2 us
    all_to_all x1, waiting for transfers between devices, body(): lax.all_to_all(fourier, ('zh', 'long'), split_axis=0, concat_axis=0, tile...  9.33 us
    all_to_all x1, starting transfers between devices, body(): lax.all_to_all(blocks, 'long', split_axis=0, concat_axis=0, tiled=True)  9.09 us
  transfers between devices with their start and end apart: 8, of which 4 were waited for; matrix products, arithmetic and copies ran while one was open for 1% of the time, Pallas kernels for 3%

profile of v4, /device:TPU:32, one launch (start us, length us, event | category | flops | bytes accessed | tf_op | source)
XLA Modules:
  0.0 177.0 jit_solution(3785023535419434400)
XLA Ops:
  0.0 2.3 %shard_map.64 = bf16[32,3,32,128]{3,2,1,0:T(8,128)(2,1)} custom-call(bf16[3,8,32,512]{3,2,1,0:T(8,128)(2,1)} %vel_ref.1, bf16[3,8,32,512]{3,2,1,0:T(8,128)(2,1)} %vort_ref.1), custom_call_target="tpu_custom_call" | custom-call | tf_op jit(solution)/shard_map/pallas_call | solution.py:38
  2.3 9.1 %all-to-all-start = ((bf16[32,3,32,128]{3,2,1,0:T(8,128)(2,1)}), bf16[32,3,32,128]{3,2,1,0:T(8,128)(2,1)S(1)}, u32[]{:S(2)}, u32[]{:S(2)}) async-start(bf16[32,3,32,128]{3,2,1,0:T(8,128)(2,1)} %shard_map.64), calls=%async_computation | async-start | bytes 1572864 | tf_op jit(solution)/shard_map/all_to_all | solution.py:223
  11.4 0.8 constant_dynamic-slice_fusion
  12.2 9.7 %collective-permute-start.2 = (bf16[4,32,512]{2,1,0:T(8,128)(2,1)}, bf16[4,32,512]{2,1,0:T(8,128)(2,1)}, u32[]{:S(2)}, u32[]{:S(2)}) collective-permute-start(bf16[4,32,512]{2,1,0:T(8,128)(2,1)} %get-tuple-element.25), channel_id=1, source_target_pairs={{0,96},{32,0},{64,32},{96,64},{1,97},{33,1},{65,33},{97,65},{2,98}... | collective-permute-start | bytes 393224 | tf_op jit(solution)/shard_map/ppermute | solution.py:212
  22.0 1.9 %collective-permute-start = (bf16[4,32,512]{2,1,0:T(8,128)(2,1)}, bf16[4,32,512]{2,1,0:T(8,128)(2,1)}, u32[]{:S(2)}, u32[]{:S(2)}) collective-permute-start(bf16[4,32,512]{2,1,0:T(8,128)(2,1)} %get-tuple-element.26), channel_id=1, source_target_pairs={{0,32},{32,64},{64,96},{96,0},{1,33},{33,65},{65,97},{97,1},{2,34}... | collective-permute-start | bytes 393224 | tf_op jit(solution)/shard_map/ppermute | solution.py:212
  23.9 10.8 %collective-permute-start.1 = (bf16[4,32,512]{2,1,0:T(8,128)(2,1)}, bf16[4,32,512]{2,1,0:T(8,128)(2,1)}, u32[]{:S(2)}, u32[]{:S(2)}) collective-permute-start(bf16[4,32,512]{2,1,0:T(8,128)(2,1)} %get-tuple-element.28), channel_id=1, source_target_pairs={{0,64},{32,96},{64,0},{96,32},{1,65},{33,97},{65,1},{97,33},{2,66}... | collective-permute-start | bytes 393224 | tf_op jit(solution)/shard_map/ppermute | solution.py:212
  34.7 0.1 convert_element_type.24
  34.9 0.1 convert_element_type.26
  35.0 0.1 broadcast_in_dim.4
  35.1 0.2 convert_element_type.28.mode_ref
  35.3 5.6 %shard_map.65.table_ref = bf16[1024,1024]{1,0:T(8,128)(2,1)S(1)} custom-call(f32[1024,1]{1,0:T(8,128)S(1)} %convert_element_type.28.mode_ref), custom_call_target="tpu_custom_call" | custom-call | tf_op jit(solution)/shard_map/pallas_call | solution.py:69
  40.9 0.0 collective-permute-done.2
  40.9 18.7 %collective-permute-done = bf16[4,32,512]{2,1,0:T(8,128)(2,1)} collective-permute-done((bf16[4,32,512]{2,1,0:T(8,128)(2,1)}, bf16[4,32,512]{2,1,0:T(8,128)(2,1)}, u32[]{:S(2)}, u32[]{:S(2)}) %collective-permute-start) | collective-permute-done | bytes 131104 | tf_op jit(solution)/shard_map/ppermute | solution.py:212
  59.6 0.0 collective-permute-done.1
  59.6 1.7 shard_map.66
  61.4 0.0 copy-start
  61.4 0.9 copy-done
  62.2 11.2 %all-to-all-start.1 = ((bf16[128,8,384]{2,1,0:T(8,128)(2,1)}), bf16[128,8,384]{2,1,0:T(8,128)(2,1)S(1)}, u32[]{:S(2)}, u32[]{:S(2)}) async-start(bf16[128,8,384]{2,1,0:T(8,128)(2,1)} %bitcast.12), calls=%async_computation.1 | async-start | bytes 1572864 | tf_op jit(solution)/shard_map/all_to_all | solution.py:229
  73.4 1.1 pad_maximum_fusion.leg0_ref
  74.5 4.7 %collective-permute-start.5 = (bf16[4,4,32,512]{3,2,1,0:T(8,128)(2,1)S(1)}, bf16[4,4,32,512]{3,2,1,0:T(8,128)(2,1)S(1)}, u32[]{:S(2)}, u32[]{:S(2)}) collective-permute-start(bf16[4,4,32,512]{3,2,1,0:T(8,128)(2,1)S(1)} %pad_maximum_fusion.leg0_ref), channel_id=1, source_target_pairs={{0,384},{128,0},{256,128},{384,256},{1,385},{129,1},{257,129},{385... | collective-permute-start | bytes 1572872 | tf_op jit(solution)/shard_map/ppermute | solution.py:226
  79.2 2.7 %collective-permute-start.4 = (bf16[4,4,32,512]{3,2,1,0:T(8,128)(2,1)S(1)}, bf16[4,4,32,512]{3,2,1,0:T(8,128)(2,1)S(1)}, u32[]{:S(2)}, u32[]{:S(2)}) collective-permute-start(bf16[4,4,32,512]{3,2,1,0:T(8,128)(2,1)S(1)} %pad_maximum_fusion.leg0_ref), channel_id=1, source_target_pairs={{0,256},{128,384},{256,0},{384,128},{1,257},{129,385},{257,1},{385... | collective-permute-start | bytes 1572872 | tf_op jit(solution)/shard_map/ppermute | solution.py:226
  81.9 2.8 %collective-permute-start.3 = (bf16[4,4,32,512]{3,2,1,0:T(8,128)(2,1)S(1)}, bf16[4,4,32,512]{3,2,1,0:T(8,128)(2,1)S(1)}, u32[]{:S(2)}, u32[]{:S(2)}) collective-permute-start(bf16[4,4,32,512]{3,2,1,0:T(8,128)(2,1)S(1)} %pad_maximum_fusion.leg0_ref), channel_id=1, source_target_pairs={{0,128},{128,256},{256,384},{384,0},{1,129},{129,257},{257,385},{3... | collective-permute-start | bytes 1572872 | tf_op jit(solution)/shard_map/ppermute | solution.py:226
  84.7 0.1 pad_add_fusion.place_ref
  84.8 17.1 %collective-permute-done.5.leg3_ref = bf16[4,4,32,512]{3,2,1,0:T(8,128)(2,1)S(1)} collective-permute-done((bf16[4,4,32,512]{3,2,1,0:T(8,128)(2,1)S(1)}, bf16[4,4,32,512]{3,2,1,0:T(8,128)(2,1)S(1)}, u32[]{:S(2)}, u32[]{:S(2)}) %collective-permute-start.5) | collective-permute-done | bytes 524320 | tf_op jit(solution)/shard_map/ppermute | solution.py:226
  102.0 0.0 collective-permute-done.4.leg2_ref
  102.0 5.6 %collective-permute-done.3.leg1_ref = bf16[4,4,32,512]{3,2,1,0:T(8,128)(2,1)S(1)} collective-permute-done((bf16[4,4,32,512]{3,2,1,0:T(8,128)(2,1)S(1)}, bf16[4,4,32,512]{3,2,1,0:T(8,128)(2,1)S(1)}, u32[]{:S(2)}, u32[]{:S(2)}) %collective-permute-start.3) | collective-permute-done | bytes 524320 | tf_op jit(solution)/shard_map/ppermute | solution.py:226
  107.5 0.8 copy-done.3
  108.3 9.3 %all-to-all-done.1 = bf16[128,8,384]{2,1,0:T(8,128)(2,1)S(1)} async-done(((bf16[128,8,384]{2,1,0:T(8,128)(2,1)}), bf16[128,8,384]{2,1,0:T(8,128)(2,1)S(1)}, u32[]{:S(2)}, u32[]{:S(2)}) %all-to-all-start.1) | async-done | bytes 786464 | tf_op jit(solution)/shard_map/all_to_all | solution.py:229
  117.7 1.0 copy-done.4
  118.7 2.9 %shard_map.67 = bf16[16,2,32,384]{3,2,1,0:T(8,128)(2,1)S(1)} custom-call(s32[2]{0:T(128)S(1)} %pad_add_fusion.place_ref, bf16[1024,384]{1,0:T(8,128)(2,1)S(1)} %bitcast.13, bf16[4,4,32,512]{3,2,1,0:T(8,128)(2,1)S(1)} %pad_maximum_fusion.leg0_ref, bf16[4,4,32,512]{3,2,1,0:T(8,128)(2,1)S(1)} %copy-done.4, ...), custom_call_target="tpu_custom_call" | custom-call | tf_op jit(solution)/shard_map/pallas_call | solution.py:148
  121.6 52.1 %all_to_all.15 = bf16[16,2,32,384]{3,2,1,0:T(8,128)(2,1)S(1)} all-to-all(bf16[16,2,32,384]{3,2,1,0:T(8,128)(2,1)S(1)} %shard_map.67), channel_id=1, replica_groups=mesh['x'=4,'zh'=4,'long'=32] {'x','zh'}, dimensions={0} | all-to-all | bytes 1572864 | tf_op jit(solution)/shard_map/all_to_all | solution.py:231
  173.7 3.2 %shard_map.68 = bf16[8,2,6,32,128]{4,3,2,1,0:T(8,128)(2,1)} custom-call(bf16[4,8,32,384]{3,2,1,0:T(8,128)(2,1)S(1)} %bitcast.14, bf16[8,2,6,32,128]{4,3,2,1,0:T(8,128)(2,1)S(1)} %bitcast.15, bf16[32,128,128]{2,1,0:T(8,128)(2,1)S(1)} %copy-done.1), custom_call_target="tpu_custom_call" | custom-call | tf_op jit(solution)/shard_map/pallas_call | solution.py:199
  (13 shorter events, 0.0 us)
Async XLA Ops:
  0.0 11.4 %copy-start.5 = (bf16[16,32,512]{2,1,0:T(8,128)(2,1)S(1)}, bf16[16,32,512]{2,1,0:T(8,128)(2,1)}, u32[]{:S(2)}) copy-start(bf16[16,32,512]{2,1,0:T(8,128)(2,1)} %param.9) | copy-start | bytes 1572868
  0.0 34.7 %copy-start.6 = (s32[512]{0:T(512)S(1)}, s32[512]{0:T(512)}, u32[]{:S(2)}) copy-start(s32[512]{0:T(512)} %param.8) | copy-start | bytes 6148
  2.3 57.3 %all-to-all-start = ((bf16[32,3,32,128]{3,2,1,0:T(8,128)(2,1)}), bf16[32,3,32,128]{3,2,1,0:T(8,128)(2,1)S(1)}, u32[]{:S(2)}, u32[]{:S(2)}) async-start(bf16[32,3,32,128]{3,2,1,0:T(8,128)(2,1)} %shard_map.64), calls=%async_computation | async-start | bytes 1572864 | tf_op jit(solution)/shard_map/all_to_all | solution.py:223
  12.2 28.7 %collective-permute-start.2 = (bf16[4,32,512]{2,1,0:T(8,128)(2,1)}, bf16[4,32,512]{2,1,0:T(8,128)(2,1)}, u32[]{:S(2)}, u32[]{:S(2)}) collective-permute-start(bf16[4,32,512]{2,1,0:T(8,128)(2,1)} %get-tuple-element.25), channel_id=1, source_target_pairs={{0,96},{32,0},{64,32},{96,64},{1,97},{33,1},{65,33},{97,65},{2,98}... | collective-permute-start | bytes 393224 | tf_op jit(solution)/shard_map/ppermute | solution.py:212
  22.0 37.7 %collective-permute-start = (bf16[4,32,512]{2,1,0:T(8,128)(2,1)}, bf16[4,32,512]{2,1,0:T(8,128)(2,1)}, u32[]{:S(2)}, u32[]{:S(2)}) collective-permute-start(bf16[4,32,512]{2,1,0:T(8,128)(2,1)} %get-tuple-element.26), channel_id=1, source_target_pairs={{0,32},{32,64},{64,96},{96,0},{1,33},{33,65},{65,97},{97,1},{2,34}... | collective-permute-start | bytes 393224 | tf_op jit(solution)/shard_map/ppermute | solution.py:212
  23.9 35.7 %collective-permute-start.1 = (bf16[4,32,512]{2,1,0:T(8,128)(2,1)}, bf16[4,32,512]{2,1,0:T(8,128)(2,1)}, u32[]{:S(2)}, u32[]{:S(2)}) collective-permute-start(bf16[4,32,512]{2,1,0:T(8,128)(2,1)} %get-tuple-element.28), channel_id=1, source_target_pairs={{0,64},{32,96},{64,0},{96,32},{1,65},{33,97},{65,1},{97,33},{2,66}... | collective-permute-start | bytes 393224 | tf_op jit(solution)/shard_map/ppermute | solution.py:212
  61.4 0.9 copy-start
  62.2 55.4 %all-to-all-start.1 = ((bf16[128,8,384]{2,1,0:T(8,128)(2,1)}), bf16[128,8,384]{2,1,0:T(8,128)(2,1)S(1)}, u32[]{:S(2)}, u32[]{:S(2)}) async-start(bf16[128,8,384]{2,1,0:T(8,128)(2,1)} %bitcast.12), calls=%async_computation.1 | async-start | bytes 1572864 | tf_op jit(solution)/shard_map/all_to_all | solution.py:229
  74.5 27.4 %collective-permute-start.5 = (bf16[4,4,32,512]{3,2,1,0:T(8,128)(2,1)S(1)}, bf16[4,4,32,512]{3,2,1,0:T(8,128)(2,1)S(1)}, u32[]{:S(2)}, u32[]{:S(2)}) collective-permute-start(bf16[4,4,32,512]{3,2,1,0:T(8,128)(2,1)S(1)} %pad_maximum_fusion.leg0_ref), channel_id=1, source_target_pairs={{0,384},{128,0},{256,128},{384,256},{1,385},{129,1},{257,129},{385... | collective-permute-start | bytes 1572872 | tf_op jit(solution)/shard_map/ppermute | solution.py:226
  79.2 22.7 %collective-permute-start.4 = (bf16[4,4,32,512]{3,2,1,0:T(8,128)(2,1)S(1)}, bf16[4,4,32,512]{3,2,1,0:T(8,128)(2,1)S(1)}, u32[]{:S(2)}, u32[]{:S(2)}) collective-permute-start(bf16[4,4,32,512]{3,2,1,0:T(8,128)(2,1)S(1)} %pad_maximum_fusion.leg0_ref), channel_id=1, source_target_pairs={{0,256},{128,384},{256,0},{384,128},{1,257},{129,385},{257,1},{385... | collective-permute-start | bytes 1572872 | tf_op jit(solution)/shard_map/ppermute | solution.py:226
  81.9 25.6 %collective-permute-start.3 = (bf16[4,4,32,512]{3,2,1,0:T(8,128)(2,1)S(1)}, bf16[4,4,32,512]{3,2,1,0:T(8,128)(2,1)S(1)}, u32[]{:S(2)}, u32[]{:S(2)}) collective-permute-start(bf16[4,4,32,512]{3,2,1,0:T(8,128)(2,1)S(1)} %pad_maximum_fusion.leg0_ref), channel_id=1, source_target_pairs={{0,128},{128,256},{256,384},{384,0},{1,129},{129,257},{257,385},{3... | collective-permute-start | bytes 1572872 | tf_op jit(solution)/shard_map/ppermute | solution.py:226
  107.5 0.8 copy-start.3
  117.7 1.0 copy-start.4
  118.7 55.0 %copy-start.1 = (bf16[32,128,128]{2,1,0:T(8,128)(2,1)S(1)}, bf16[32,128,128]{2,1,0:T(8,128)(2,1)}, u32[]{:S(2)}) copy-start(bf16[32,128,128]{2,1,0:T(8,128)(2,1)} %inverse_ref.1) | copy-start | bytes 3145732
  118.7 55.0 %copy-start.2 = (bf16[16,2,3,32,128]{4,3,2,1,0:T(8,128)(2,1)S(1)}, bf16[16,2,3,32,128]{4,3,2,1,0:T(8,128)(2,1)}, u32[]{:S(2)}) copy-start(bf16[16,2,3,32,128]{4,3,2,1,0:T(8,128)(2,1)} %param.10) | copy-start | bytes 2359300

commit v5 on v4

--- a/solution.py
+++ b/solution.py
@@ -62,9 +62,8 @@
     out_ref[...] = (value * quarter).astype(jnp.bfloat16)
 
 
-def phase_rows(m_of_slot, points, groups, subs):
-    modes = m_of_slot.reshape(-1, groups, subs).transpose(1, 0, 2).reshape(-1)
-    paired = jnp.repeat(modes, 2).astype(jnp.float32)[:, None]
+def phase_rows(m_of_slot, points):
+    paired = jnp.repeat(m_of_slot, 2).astype(jnp.float32)[:, None]
     rows, step = paired.shape[0], 256
     return pl.pallas_call(
         phase_kernel,
@@ -115,8 +114,8 @@
         k = pair * 2 + kk
 
         def source(i):
-            tb, c, z, r = i // 32, (i // 16) % 2, (i // 8) % 2, i % 8
-            return ((z * 8 + r) * 4 + tb) * 8 + k * 2 + c
+            tb, c, z, r = i // 32, (i // 16) % 2, (i // 4) % 4, i % 4
+            return ((r * 4 + tb) * 4 + z) * 8 + k * 2 + c
 
         move = matches(source, (128, 512))
         for h in range(2):
@@ -140,7 +139,7 @@
         ]
         both = jnp.concatenate(coeffs, axis=1)
         for d in range(4):
-            out_ref[((place_x - e) & 3) * 4 + ((zh - d) & 3), 0] = both[d * 32 : (d + 1) * 32, :]
+            out_ref[((zh - d) & 3) * 4 + ((place_x - e - place_ref[2 + d]) & 3), 0] = both[d * 32 : (d + 1) * 32, :]
 
 
 def legendre_step(place, y, legs):
@@ -162,12 +161,15 @@
 
 def solve_kernel(coeffs_ref, known_ref, inverse_ref, out_ref, side, solved):
     nr = known_ref.shape[-1]
-    lanes = matches(lambda i: ((i // 32) % 4) * 128 + (i // 128) * 32 + i % 32, (512, 512))
+    lanes = matches(
+        lambda i: ((i // 32) % 4) * 128 + (i // 128) * 32 + ((i // 4) % 4) * 8 + ((i // 16) % 2) * 4 + i % 4,
+        (512, 512),
+    )
     swap = matches(lambda i: (i % 16) * 16 + i // 16, (256, 256))
     grouped = []
     for g in range(3):
         wide = jnp.concatenate(
-            [coeffs_ref[x, :, :, g * LANES : (g + 1) * LANES].reshape(256, LANES) for x in range(4)], axis=1
+            [coeffs_ref[:, x, :, :, g * LANES : (g + 1) * LANES].reshape(256, LANES) for x in range(4)], axis=1
         )
         grouped.append(jnp.dot(wide, lanes, preferred_element_type=jnp.float32).astype(jnp.bfloat16))
     for cf in range(6):
@@ -204,34 +206,62 @@
     )(coeffs, known, inverse)
 
 
+def live(x, zh, long):
+    last_degree = (x * 4 + zh) * 32 + 31
+    return last_degree >= long * 16 - 31
+
+
+def aside(zl):
+    return ((0, 0, 0, 0), (0, 0, 0, 0), (0, 0, 2, 0), (0, 1, 1, 1))[zl]
+
+
+def send_live(array, axis, shift):
+    pairs = []
+    for x in range(4):
+        for zh in range(4):
+            for long in range(32):
+                off = aside(long // 8)
+                if axis == "x":
+                    to = ((x + shift) % 4 * 4 + zh) * 32 + long
+                    sent = any(live((x - off[d]) % 4, (zh - d) % 4, long) for d in range(4))
+                else:
+                    to = ((x + off[shift]) % 4 * 4 + (zh + shift) % 4) * 32 + long
+                    sent = live(x, zh, long)
+                if sent:
+                    pairs.append(((x * 4 + zh) * 32 + long, to))
+    return lax.ppermute(array, ("x", "zh", "long"), pairs)
+
+
 def legendre_by_slot(legendre, zh):
     pieces = []
     for d in range(4):
         piece = lax.dynamic_slice_in_dim(legendre, ((zh + d) & 3) * 4, 4, axis=0)
         if d:
-            piece = lax.ppermute(piece, "zh", [(i, (i + d) % 4) for i in range(4)])
+            piece = send_live(piece, "zh", d)
         pieces.append(piece)
     return pieces
 
 
 def body(velocity, vorticity, m_of_slot, legendre, known_term, inverse):
     place_x, zh = lax.axis_index("x"), lax.axis_index("zh")
-    table = phase_rows(m_of_slot, velocity.shape[2] * 32, 4, 4)
+    table = phase_rows(m_of_slot, velocity.shape[2] * 32)
     pieces = legendre_by_slot(legendre, zh)
+    aside_here = jnp.array([aside(zl) for zl in range(4)], jnp.int32)[lax.axis_index("long") // 8]
+    place = jnp.concatenate([jnp.stack([place_x, zh]), aside_here])
     table, *pieces = lax.optimization_barrier((table, *pieces))
     blocks = lamb_blocks(velocity, vorticity)
     blocks = lax.all_to_all(blocks, "long", split_axis=0, concat_axis=0, tiled=True)
     blocks, *pieces = lax.optimization_barrier((blocks, *pieces))
     leg = jnp.stack(pieces, axis=0)
-    legs = [leg] + [lax.ppermute(leg, "x", [(i, (i + e) % 4) for i in range(4)]) for e in (1, 2, 3)]
+    legs = [leg] + [send_live(leg, "x", e) for e in (1, 2, 3)]
     fourier = dft(blocks, table)
     fourier = fourier.reshape(-1, 8, 3 * LANES)
-    fourier = lax.all_to_all(fourier, ("zh", "long"), split_axis=0, concat_axis=0, tiled=True)
-    coeffs = legendre_step(jnp.stack([place_x, zh]), fourier.reshape(-1, 3 * LANES), legs)
-    coeffs = lax.all_to_all(coeffs, ("x", "zh"), split_axis=0, concat_axis=0, tiled=True)
+    fourier = lax.all_to_all(fourier, ("long", "zh"), split_axis=0, concat_axis=0, tiled=True)
+    coeffs = legendre_step(place, fourier.reshape(-1, 3 * LANES), legs)
+    coeffs = lax.all_to_all(coeffs, ("zh", "x"), split_axis=0, concat_axis=0, tiled=True)
     nr = known_term.shape[-1]
     solved = radial_solve(
-        coeffs.reshape(4, 8, 32, 384), known_term.reshape(8, 2, 6, 32, nr), inverse
+        coeffs.reshape(4, 4, 2, 32, 384), known_term.reshape(8, 2, 6, 32, nr), inverse
     )
     return solved.reshape(known_term.shape)
 

time: 178 us -> 175 us (0.983)
  starting transfers between devices: 52.9 us -> 44.9 us
  waiting for transfers between devices: 50.8 us -> 56.3 us
  blocking collectives: 52.1 us -> 53.9 us
    ppermute x6, starting transfers between devices: 32.6 us -> 15.2 us  [send_live(): return lax.ppermute(array, ('x', 'zh', 'long'), pairs)]
    all_to_all x1, starting transfers between devices: 11.2 us -> 20.6 us  [body(): lax.all_to_all(fourier, ('long', 'zh'), split_axis=0, concat_axis=0, tile...]
    ppermute x6, waiting for transfers between devices: 41.5 us -> 49.2 us  [send_live(): return lax.ppermute(array, ('x', 'zh', 'long'), pairs)]
    all_to_all x1, waiting for transfers between devices: 9.33 us -> 7.15 us  [body(): lax.all_to_all(fourier, ('long', 'zh'), split_axis=0, concat_axis=0, tile...]
    unnamed x14 -> x10, local copies, waits for them, and re-layouts: 2.72 us -> 0.89 us
    all_to_all x1, blocking collectives: 52.1 us -> 53.9 us  [body(): lax.all_to_all(coeffs, ('zh', 'x'), split_axis=0, concat_axis=0, tiled=True)]
  transfers between devices with their start and end apart: 8 -> 8, of which waited for: 4 -> 4; matrix products, arithmetic and copies ran while one was open for 1% -> 2% of each run, Pallas kernels for 3% -> 3%
where the time goes in v5:
time: 175 us
  waiting for transfers between devices  56.3 us (32%)
  blocking collectives  53.9 us (31%)
  starting transfers between devices  44.9 us (26%)
  Pallas kernels  15.8 us (9%)
  local copies, waits for them, and re-layouts  2.64 us (2%)
    all_to_all x1, blocking collectives, body(): lax.all_to_all(coeffs, ('zh', 'x'), split_axis=0, concat_axis=0, tiled=True)  53.9 us
    ppermute x6, waiting for transfers between devices, send_live(): return lax.ppermute(array, ('x', 'zh', 'long'), pairs)  49.2 us
    all_to_all x1, starting transfers between devices, body(): lax.all_to_all(fourier, ('long', 'zh'), split_axis=0, concat_axis=0, tile...  20.6 us
    ppermute x6, starting transfers between devices, send_live(): return lax.ppermute(array, ('x', 'zh', 'long'), pairs)  15.2 us
    all_to_all x1, starting transfers between devices, body(): lax.all_to_all(blocks, 'long', split_axis=0, concat_axis=0, tiled=True)  9.09 us
    all_to_all x1, waiting for transfers between devices, body(): lax.all_to_all(fourier, ('long', 'zh'), split_axis=0, concat_axis=0, tile...  7.15 us
    pallas_call x1, Pallas kernels, phase_rows(): pl.pallas_call(phase_kernel, grid=(rows // step,), in_specs=[pl.BlockSpec...  5.58 us
  transfers between devices with their start and end apart: 8, of which 4 were waited for; matrix products, arithmetic and copies ran while one was open for 2% of the time, Pallas kernels for 3%

profile of v5, /device:TPU:32, one launch (start us, length us, event | category | flops | bytes accessed | tf_op | source)
XLA Modules:
  0.0 174.9 jit_solution(1228499493751545100)
XLA Ops:
  0.0 2.3 %shard_map.73 = bf16[32,3,32,128]{3,2,1,0:T(8,128)(2,1)} custom-call(bf16[3,8,32,512]{3,2,1,0:T(8,128)(2,1)} %vel_ref.1, bf16[3,8,32,512]{3,2,1,0:T(8,128)(2,1)} %vort_ref.1), custom_call_target="tpu_custom_call" | custom-call | tf_op jit(solution)/shard_map/pallas_call | solution.py:38
  2.3 9.1 %all-to-all-start = ((bf16[32,3,32,128]{3,2,1,0:T(8,128)(2,1)}), bf16[32,3,32,128]{3,2,1,0:T(8,128)(2,1)S(1)}, u32[]{:S(2)}, u32[]{:S(2)}) async-start(bf16[32,3,32,128]{3,2,1,0:T(8,128)(2,1)} %shard_map.73), calls=%async_computation | async-start | bytes 1572864 | tf_op jit(solution)/shard_map/all_to_all | solution.py:253
  11.4 0.8 constant_dynamic-slice_fusion
  12.2 1.3 collective-permute-start.2
  13.5 1.3 collective-permute-start
  14.8 1.3 collective-permute-start.1
  16.1 0.0 copy-done.4
  16.1 0.1 broadcast_in_dim.4
  16.2 0.2 convert_element_type.16.mode_ref
  16.4 5.6 %shard_map.74.table_ref = bf16[1024,1024]{1,0:T(8,128)(2,1)S(1)} custom-call(f32[1024,1]{1,0:T(8,128)S(1)} %convert_element_type.16.mode_ref), custom_call_target="tpu_custom_call" | custom-call | tf_op jit(solution)/shard_map/pallas_call | solution.py:68
  22.0 0.0 collective-permute-done.2
  22.0 26.3 %collective-permute-done = bf16[4,32,512]{2,1,0:T(8,128)(2,1)} collective-permute-done((bf16[4,32,512]{2,1,0:T(8,128)(2,1)}, bf16[4,32,512]{2,1,0:T(8,128)(2,1)}, u32[]{:S(2)}, u32[]{:S(2)}) %collective-permute-start) | collective-permute-done | bytes 131104 | tf_op jit(solution)/shard_map/ppermute | solution.py:232
  48.3 0.0 collective-permute-done.1
  48.3 0.0 all-to-all-done.x_ref
  48.3 1.7 shard_map.75
  50.1 0.0 copy-start
  50.1 0.9 copy-done
  51.0 20.6 %all-to-all-start.1 = ((bf16[128,8,384]{2,1,0:T(8,128)(2,1)}), bf16[128,8,384]{2,1,0:T(8,128)(2,1)S(1)}, u32[]{:S(2)}, u32[]{:S(2)}) async-start(bf16[128,8,384]{2,1,0:T(8,128)(2,1)} %bitcast.13), calls=%async_computation.1 | async-start | bytes 1572864 | tf_op jit(solution)/shard_map/all_to_all | solution.py:259
  71.6 1.1 pad_maximum_fusion.leg0_ref
  72.7 6.6 %collective-permute-start.5 = (bf16[4,4,32,512]{3,2,1,0:T(8,128)(2,1)S(1)}, bf16[4,4,32,512]{3,2,1,0:T(8,128)(2,1)S(1)}, u32[]{:S(2)}, u32[]{:S(2)}) collective-permute-start(bf16[4,4,32,512]{3,2,1,0:T(8,128)(2,1)S(1)} %pad_maximum_fusion.leg0_ref), channel_id=1, source_target_pairs={{0,384},{1,385},{2,386},{3,387},{4,388},{5,389},{6,390},{7,391},{8... | collective-permute-start | bytes 1572872 | tf_op jit(solution)/shard_map/ppermute | solution.py:232
  79.3 1.9 %collective-permute-start.4 = (bf16[4,4,32,512]{3,2,1,0:T(8,128)(2,1)S(1)}, bf16[4,4,32,512]{3,2,1,0:T(8,128)(2,1)S(1)}, u32[]{:S(2)}, u32[]{:S(2)}) collective-permute-start(bf16[4,4,32,512]{3,2,1,0:T(8,128)(2,1)S(1)} %pad_maximum_fusion.leg0_ref), channel_id=1, source_target_pairs={{0,256},{1,257},{2,258},{3,259},{4,260},{5,261},{6,262},{7,263},{8... | collective-permute-start | bytes 1572872 | tf_op jit(solution)/shard_map/ppermute | solution.py:232
  81.2 2.8 %collective-permute-start.3 = (bf16[4,4,32,512]{3,2,1,0:T(8,128)(2,1)S(1)}, bf16[4,4,32,512]{3,2,1,0:T(8,128)(2,1)S(1)}, u32[]{:S(2)}, u32[]{:S(2)}) collective-permute-start(bf16[4,4,32,512]{3,2,1,0:T(8,128)(2,1)S(1)} %pad_maximum_fusion.leg0_ref), channel_id=1, source_target_pairs={{0,128},{1,129},{2,130},{3,131},{4,132},{5,133},{6,134},{7,135},{8... | collective-permute-start | bytes 1572872 | tf_op jit(solution)/shard_map/ppermute | solution.py:232
  84.0 0.7 fusion
  84.7 0.1 pad_add_fusion.place_ref
  84.8 17.2 %collective-permute-done.5.leg3_ref = bf16[4,4,32,512]{3,2,1,0:T(8,128)(2,1)S(1)} collective-permute-done((bf16[4,4,32,512]{3,2,1,0:T(8,128)(2,1)S(1)}, bf16[4,4,32,512]{3,2,1,0:T(8,128)(2,1)S(1)}, u32[]{:S(2)}, u32[]{:S(2)}) %collective-permute-start.5) | collective-permute-done | bytes 524320 | tf_op jit(solution)/shard_map/ppermute | solution.py:232
  102.0 0.0 collective-permute-done.4.leg2_ref
  102.0 5.6 %collective-permute-done.3.leg1_ref = bf16[4,4,32,512]{3,2,1,0:T(8,128)(2,1)S(1)} collective-permute-done((bf16[4,4,32,512]{3,2,1,0:T(8,128)(2,1)S(1)}, bf16[4,4,32,512]{3,2,1,0:T(8,128)(2,1)S(1)}, u32[]{:S(2)}, u32[]{:S(2)}) %collective-permute-start.3) | collective-permute-done | bytes 524320 | tf_op jit(solution)/shard_map/ppermute | solution.py:232
  107.6 7.1 %all-to-all-done.1 = bf16[128,8,384]{2,1,0:T(8,128)(2,1)S(1)} async-done(((bf16[128,8,384]{2,1,0:T(8,128)(2,1)}), bf16[128,8,384]{2,1,0:T(8,128)(2,1)S(1)}, u32[]{:S(2)}, u32[]{:S(2)}) %all-to-all-start.1) | async-done | bytes 786464 | tf_op jit(solution)/shard_map/all_to_all | solution.py:259
  114.8 2.9 %shard_map.76 = bf16[16,2,32,384]{3,2,1,0:T(8,128)(2,1)S(1)} custom-call(s32[6]{0:T(128)S(1)} %pad_add_fusion.place_ref, bf16[1024,384]{1,0:T(8,128)(2,1)S(1)} %bitcast.14, bf16[4,4,32,512]{3,2,1,0:T(8,128)(2,1)S(1)} %pad_maximum_fusion.leg0_ref, bf16[4,4,32,512]{3,2,1,0:T(8,128)(2,1)S(1)} %collective-permute-done.3.leg1_ref, ...), custom_call_target="tpu_custom_call" | custom-call | tf_op jit(solution)/shard_map/pallas_call | solution.py:147
  117.7 53.9 %all_to_all.15 = bf16[16,2,32,384]{3,2,1,0:T(8,128)(2,1)S(1)} all-to-all(bf16[16,2,32,384]{3,2,1,0:T(8,128)(2,1)S(1)} %shard_map.76), channel_id=1, replica_groups=mesh['x'=4,'zh'=4,'long'=32] {'zh','x'}, dimensions={0} | all-to-all | bytes 1572864 | tf_op jit(solution)/shard_map/all_to_all | solution.py:261
  171.6 0.0 copy-done.1
  171.6 3.3 %shard_map.77 = bf16[8,2,6,32,128]{4,3,2,1,0:T(8,128)(2,1)} custom-call(bf16[4,4,2,32,384]{4,3,2,1,0:T(8,128)(2,1)S(1)} %bitcast.15, bf16[8,2,6,32,128]{4,3,2,1,0:T(8,128)(2,1)S(1)} %bitcast.16, bf16[32,128,128]{2,1,0:T(8,128)(2,1)S(1)} %copy-done.1), custom_call_target="tpu_custom_call" | custom-call | tf_op jit(solution)/shard_map/pallas_call | solution.py:201
  (7 shorter events, 0.0 us)
Async XLA Ops:
  0.0 11.4 %copy-start.3 = (bf16[16,32,512]{2,1,0:T(8,128)(2,1)S(1)}, bf16[16,32,512]{2,1,0:T(8,128)(2,1)}, u32[]{:S(2)}) copy-start(bf16[16,32,512]{2,1,0:T(8,128)(2,1)} %param.10) | copy-start | bytes 1572868
  0.0 16.1 %copy-start.4 = (s32[512]{0:T(512)S(1)}, s32[512]{0:T(512)}, u32[]{:S(2)}) copy-start(s32[512]{0:T(512)} %param.9) | copy-start | bytes 6148
  2.3 46.0 %all-to-all-start = ((bf16[32,3,32,128]{3,2,1,0:T(8,128)(2,1)}), bf16[32,3,32,128]{3,2,1,0:T(8,128)(2,1)S(1)}, u32[]{:S(2)}, u32[]{:S(2)}) async-start(bf16[32,3,32,128]{3,2,1,0:T(8,128)(2,1)} %shard_map.73), calls=%async_computation | async-start | bytes 1572864 | tf_op jit(solution)/shard_map/all_to_all | solution.py:253
  12.2 9.8 %collective-permute-start.2 = (bf16[4,32,512]{2,1,0:T(8,128)(2,1)}, bf16[4,32,512]{2,1,0:T(8,128)(2,1)}, u32[]{:S(2)}, u32[]{:S(2)}) collective-permute-start(bf16[4,32,512]{2,1,0:T(8,128)(2,1)} %get-tuple-element.25), channel_id=1, source_target_pairs={{0,96},{1,97},{2,98},{3,99},{32,0},{33,1},{34,2},{35,3},{36,4},{37... | collective-permute-start | bytes 393224 | tf_op jit(solution)/shard_map/ppermute | solution.py:232
  13.5 34.8 %collective-permute-start = (bf16[4,32,512]{2,1,0:T(8,128)(2,1)}, bf16[4,32,512]{2,1,0:T(8,128)(2,1)}, u32[]{:S(2)}, u32[]{:S(2)}) collective-permute-start(bf16[4,32,512]{2,1,0:T(8,128)(2,1)} %get-tuple-element.26), channel_id=1, source_target_pairs={{0,32},{1,33},{2,34},{3,35},{32,64},{33,65},{34,66},{35,67},{36,68... | collective-permute-start | bytes 393224 | tf_op jit(solution)/shard_map/ppermute | solution.py:232
  14.8 33.5 %collective-permute-start.1 = (bf16[4,32,512]{2,1,0:T(8,128)(2,1)}, bf16[4,32,512]{2,1,0:T(8,128)(2,1)}, u32[]{:S(2)}, u32[]{:S(2)}) collective-permute-start(bf16[4,32,512]{2,1,0:T(8,128)(2,1)} %get-tuple-element.28), channel_id=1, source_target_pairs={{0,64},{1,65},{2,66},{3,67},{32,96},{33,97},{34,98},{35,99},{36,10... | collective-permute-start | bytes 393224 | tf_op jit(solution)/shard_map/ppermute | solution.py:232
  50.1 0.9 copy-start
  51.0 63.8 %all-to-all-start.1 = ((bf16[128,8,384]{2,1,0:T(8,128)(2,1)}), bf16[128,8,384]{2,1,0:T(8,128)(2,1)S(1)}, u32[]{:S(2)}, u32[]{:S(2)}) async-start(bf16[128,8,384]{2,1,0:T(8,128)(2,1)} %bitcast.13), calls=%async_computation.1 | async-start | bytes 1572864 | tf_op jit(solution)/shard_map/all_to_all | solution.py:259
  72.7 29.3 %collective-permute-start.5 = (bf16[4,4,32,512]{3,2,1,0:T(8,128)(2,1)S(1)}, bf16[4,4,32,512]{3,2,1,0:T(8,128)(2,1)S(1)}, u32[]{:S(2)}, u32[]{:S(2)}) collective-permute-start(bf16[4,4,32,512]{3,2,1,0:T(8,128)(2,1)S(1)} %pad_maximum_fusion.leg0_ref), channel_id=1, source_target_pairs={{0,384},{1,385},{2,386},{3,387},{4,388},{5,389},{6,390},{7,391},{8... | collective-permute-start | bytes 1572872 | tf_op jit(solution)/shard_map/ppermute | solution.py:232
  79.3 22.7 %collective-permute-start.4 = (bf16[4,4,32,512]{3,2,1,0:T(8,128)(2,1)S(1)}, bf16[4,4,32,512]{3,2,1,0:T(8,128)(2,1)S(1)}, u32[]{:S(2)}, u32[]{:S(2)}) collective-permute-start(bf16[4,4,32,512]{3,2,1,0:T(8,128)(2,1)S(1)} %pad_maximum_fusion.leg0_ref), channel_id=1, source_target_pairs={{0,256},{1,257},{2,258},{3,259},{4,260},{5,261},{6,262},{7,263},{8... | collective-permute-start | bytes 1572872 | tf_op jit(solution)/shard_map/ppermute | solution.py:232
  81.2 26.4 %collective-permute-start.3 = (bf16[4,4,32,512]{3,2,1,0:T(8,128)(2,1)S(1)}, bf16[4,4,32,512]{3,2,1,0:T(8,128)(2,1)S(1)}, u32[]{:S(2)}, u32[]{:S(2)}) collective-permute-start(bf16[4,4,32,512]{3,2,1,0:T(8,128)(2,1)S(1)} %pad_maximum_fusion.leg0_ref), channel_id=1, source_target_pairs={{0,128},{1,129},{2,130},{3,131},{4,132},{5,133},{6,134},{7,135},{8... | collective-permute-start | bytes 1572872 | tf_op jit(solution)/shard_map/ppermute | solution.py:232
  114.8 56.8 %copy-start.1 = (bf16[32,128,128]{2,1,0:T(8,128)(2,1)S(1)}, bf16[32,128,128]{2,1,0:T(8,128)(2,1)}, u32[]{:S(2)}) copy-start(bf16[32,128,128]{2,1,0:T(8,128)(2,1)} %inverse_ref.1) | copy-start | bytes 3145732
  114.8 56.8 %copy-start.2 = (bf16[16,2,3,32,128]{4,3,2,1,0:T(8,128)(2,1)S(1)}, bf16[16,2,3,32,128]{4,3,2,1,0:T(8,128)(2,1)}, u32[]{:S(2)}) copy-start(bf16[16,2,3,32,128]{4,3,2,1,0:T(8,128)(2,1)} %param.11) | copy-start | bytes 2359300

commit v6 on v5

--- a/solution.py
+++ b/solution.py
@@ -78,27 +78,29 @@
 def dft_kernel(x_ref, table_ref, out_ref):
     points = table_ref.shape[1]
     grid = jnp.concatenate([x_ref[:, f].reshape(points, LANES) for f in range(3)], axis=1)
-    out_ref[...] = jnp.dot(table_ref[...], grid, preferred_element_type=jnp.float32).astype(jnp.bfloat16)
+    step = 256
+
+    @pl.loop(0, table_ref.shape[0] // step)
+    def _(i):
+        rows = pl.ds(pl.multiple_of(i * step, step), step)
+        out_ref[rows, :] = jnp.dot(
+            table_ref[rows, :], grid, preferred_element_type=jnp.float32
+        ).astype(jnp.bfloat16)
 
 
 def dft(x, table):
-    rows, points = table.shape
-    step = 256
+    rows = table.shape[0]
     return pl.pallas_call(
         dft_kernel,
-        grid=(rows // step,),
-        in_specs=[
-            pl.BlockSpec(x.shape, lambda i: (0, 0, 0, 0)),
-            pl.BlockSpec((step, points), lambda i: (i, 0)),
-        ],
-        out_specs=pl.BlockSpec((step, 3 * LANES), lambda i: (i, 0)),
+        in_specs=[pl.BlockSpec(memory_space=pltpu.VMEM)] * 2,
+        out_specs=pl.BlockSpec(memory_space=pltpu.VMEM),
         out_shape=jax.ShapeDtypeStruct((rows, 3 * LANES), jnp.bfloat16),
         compiler_params=params(),
     )(x, table)
 
 
 def matches(source_of, shape):
-    row = lax.broadcasted_iota(jnp.int32, shape, 0)
+    row = lax.broadcasted_iota(jnp.int32, (shape[0], 1), 0)
     column = lax.broadcasted_iota(jnp.int32, shape, 1)
     return (source_of(row) == column).astype(jnp.float32).astype(jnp.bfloat16)
 
@@ -109,12 +111,11 @@
 
 def legendre_kernel(place_ref, y_ref, leg0_ref, leg1_ref, leg2_ref, leg3_ref, out_ref, side):
     place_x, zh = place_ref[0], place_ref[1]
-    pair = pl.program_id(0)
-    for kk in range(2):
-        k = pair * 2 + kk
+    for kk in range(4):
+        k, pair, odd = kk, kk // 2, kk % 2
 
         def source(i):
-            tb, c, z, r = i // 32, (i // 16) % 2, (i // 4) % 4, i % 4
+            tb, c, z, r = i >> 5, (i >> 4) & 1, (i >> 2) & 3, i & 3
             return ((r * 4 + tb) * 4 + z) * 8 + k * 2 + c
 
         move = matches(source, (128, 512))
@@ -124,35 +125,32 @@
                 for c in range(2):
                     for f in range(3):
                         start = (c * 3 + f) * 32 + h * 16
-                        side[kk, start : start + 16, tb * LANES : (tb + 1) * LANES] = moved[
+                        side[odd, start : start + 16, tb * LANES : (tb + 1) * LANES] = moved[
                             (tb * 2 + c) * 16 : (tb * 2 + c) * 16 + 16, f * LANES : (f + 1) * LANES
                         ]
-    for e, leg_ref in enumerate((leg0_ref, leg1_ref, leg2_ref, leg3_ref)):
-        coeffs = [
-            lax.dot_general(
-                leg_ref[:, kk].reshape(128, -1),
-                side[kk],
-                (((1,), (1,)), ((), ())),
-                preferred_element_type=jnp.float32,
-            ).astype(jnp.bfloat16)
-            for kk in range(2)
-        ]
-        both = jnp.concatenate(coeffs, axis=1)
-        for d in range(4):
-            out_ref[((zh - d) & 3) * 4 + ((place_x - e - place_ref[2 + d]) & 3), 0] = both[d * 32 : (d + 1) * 32, :]
+        if odd:
+            for e, leg_ref in enumerate((leg0_ref, leg1_ref, leg2_ref, leg3_ref)):
+                coeffs = [
+                    lax.dot_general(
+                        leg_ref[:, pair * 2 + i].reshape(128, -1),
+                        side[i],
+                        (((1,), (1,)), ((), ())),
+                        preferred_element_type=jnp.float32,
+                    ).astype(jnp.bfloat16)
+                    for i in range(2)
+                ]
+                both = jnp.concatenate(coeffs, axis=1)
+                for d in range(4):
+                    to = ((zh - d) & 3) * 4 + ((place_x - e - place_ref[2 + d]) & 3)
+                    out_ref[to, pair] = both[d * 32 : (d + 1) * 32, :]
 
 
 def legendre_step(place, y, legs):
     nodes = legs[0].shape[-1]
     return pl.pallas_call(
         legendre_kernel,
-        grid=(2,),
-        in_specs=[
-            pl.BlockSpec(memory_space=pltpu.SMEM),
-            pl.BlockSpec(y.shape, lambda p: (0, 0)),
-        ]
-        + [pl.BlockSpec((4, 2, 32, nodes), lambda p: (0, p, 0, 0))] * 4,
-        out_specs=pl.BlockSpec((16, 1, 32, 384), lambda p: (0, p, 0, 0)),
+        in_specs=[pl.BlockSpec(memory_space=pltpu.SMEM)] + [pl.BlockSpec(memory_space=pltpu.VMEM)] * 5,
+        out_specs=pl.BlockSpec(memory_space=pltpu.VMEM),
         out_shape=jax.ShapeDtypeStruct((16, 2, 32, 384), jnp.bfloat16),
         scratch_shapes=[pltpu.VMEM((2, 192, nodes), jnp.bfloat16)],
         compiler_params=params(),
@@ -162,10 +160,10 @@
 def solve_kernel(coeffs_ref, known_ref, inverse_ref, out_ref, side, solved):
     nr = known_ref.shape[-1]
     lanes = matches(
-        lambda i: ((i // 32) % 4) * 128 + (i // 128) * 32 + ((i // 4) % 4) * 8 + ((i // 16) % 2) * 4 + i % 4,
+        lambda i: ((i >> 5) & 3) * 128 + (i >> 7) * 32 + ((i >> 2) & 3) * 8 + ((i >> 4) & 1) * 4 + (i & 3),
         (512, 512),
     )
-    swap = matches(lambda i: (i % 16) * 16 + i // 16, (256, 256))
+    swap = matches(lambda i: (i & 15) * 16 + (i >> 4), (256, 256))
     grouped = []
     for g in range(3):
         wide = jnp.concatenate(
@@ -234,7 +232,7 @@
 
 def legendre_by_slot(legendre, zh):
     pieces = []
-    for d in range(4):
+    for d in (0, 1, 3, 2):
         piece = lax.dynamic_slice_in_dim(legendre, ((zh + d) & 3) * 4, 4, axis=0)
         if d:
             piece = send_live(piece, "zh", d)
@@ -252,7 +250,7 @@
     blocks = lamb_blocks(velocity, vorticity)
     blocks = lax.all_to_all(blocks, "long", split_axis=0, concat_axis=0, tiled=True)
     blocks, *pieces = lax.optimization_barrier((blocks, *pieces))
-    leg = jnp.stack(pieces, axis=0)
+    leg = jnp.stack([pieces[0], pieces[1], pieces[3], pieces[2]], axis=0)
     legs = [leg] + [send_live(leg, "x", e) for e in (1, 2, 3)]
     fourier = dft(blocks, table)
     fourier = fourier.reshape(-1, 8, 3 * LANES)

time: 175 us -> 175 us (level)
  blocking collectives: 53.9 us -> 55.9 us
  waiting for transfers between devices: 56.3 us -> 54.3 us
    all_to_all x1, starting transfers between devices: 20.6 us -> 18.6 us  [body(): lax.all_to_all(fourier, ('long', 'zh'), split_axis=0, concat_axis=0, tile...]
    all_to_all x1, waiting for transfers between devices: 7.15 us -> 5.15 us  [body(): lax.all_to_all(fourier, ('long', 'zh'), split_axis=0, concat_axis=0, tile...]
    ppermute x6, starting transfers between devices: 15.2 us -> 17.2 us  [send_live(): return lax.ppermute(array, ('x', 'zh', 'long'), pairs)]
    all_to_all x1, blocking collectives: 53.9 us -> 55.9 us  [body(): lax.all_to_all(coeffs, ('zh', 'x'), split_axis=0, concat_axis=0, tiled=True)]
where the time goes in v6:
time: 175 us; the launch traced here: 174 us
  blocking collectives  55.9 us (32%)
  waiting for transfers between devices  54.3 us (31%)
  starting transfers between devices  44.9 us (26%)
  Pallas kernels  15.4 us (9%)
  local copies, waits for them, and re-layouts  2.64 us (2%)
    all_to_all x1, blocking collectives, body(): lax.all_to_all(coeffs, ('zh', 'x'), split_axis=0, concat_axis=0, tiled=True)  55.9 us
    ppermute x6, waiting for transfers between devices, send_live(): return lax.ppermute(array, ('x', 'zh', 'long'), pairs)  49.2 us
    all_to_all x1, starting transfers between devices, body(): lax.all_to_all(fourier, ('long', 'zh'), split_axis=0, concat_axis=0, tile...  18.6 us
    ppermute x6, starting transfers between devices, send_live(): return lax.ppermute(array, ('x', 'zh', 'long'), pairs)  17.2 us
    all_to_all x1, starting transfers between devices, body(): lax.all_to_all(blocks, 'long', split_axis=0, concat_axis=0, tiled=True)  9.09 us
    pallas_call x1, Pallas kernels, phase_rows(): pl.pallas_call(phase_kernel, grid=(rows // step,), in_specs=[pl.BlockSpec...  5.58 us
    all_to_all x1, waiting for transfers between devices, body(): lax.all_to_all(fourier, ('long', 'zh'), split_axis=0, concat_axis=0, tile...  5.15 us
  transfers between devices with their start and end apart: 8, of which 4 were waited for; matrix products, arithmetic and copies ran while one was open for 2% of the time, Pallas kernels for 3%

profile of v6, /device:TPU:32, one launch (start us, length us, event | category | flops | bytes accessed | tf_op | source)
XLA Modules:
  0.0 174.4 jit_solution(11222750258457970056)
XLA Ops:
  0.0 2.3 %shard_map.73 = bf16[32,3,32,128]{3,2,1,0:T(8,128)(2,1)} custom-call(bf16[3,8,32,512]{3,2,1,0:T(8,128)(2,1)} %vel_ref.1, bf16[3,8,32,512]{3,2,1,0:T(8,128)(2,1)} %vort_ref.1), custom_call_target="tpu_custom_call" | custom-call | tf_op jit(solution)/shard_map/pallas_call | solution.py:38
  2.3 9.1 %all-to-all-start = ((bf16[32,3,32,128]{3,2,1,0:T(8,128)(2,1)}), bf16[32,3,32,128]{3,2,1,0:T(8,128)(2,1)S(1)}, u32[]{:S(2)}, u32[]{:S(2)}) async-start(bf16[32,3,32,128]{3,2,1,0:T(8,128)(2,1)} %shard_map.73), calls=%async_computation | async-start | bytes 1572864 | tf_op jit(solution)/shard_map/all_to_all | solution.py:251
  11.4 0.0 copy-done.3
  11.4 0.8 constant_dynamic-slice_fusion
  12.2 1.3 collective-permute-start.2
  13.5 1.3 collective-permute-start
  14.8 1.3 collective-permute-start.1
  16.1 0.1 broadcast_in_dim.4
  16.2 0.2 convert_element_type.16.mode_ref
  16.4 5.6 %shard_map.74.table_ref = bf16[1024,1024]{1,0:T(8,128)(2,1)S(1)} custom-call(f32[1024,1]{1,0:T(8,128)S(1)} %convert_element_type.16.mode_ref), custom_call_target="tpu_custom_call" | custom-call | tf_op jit(solution)/shard_map/pallas_call | solution.py:68
  22.0 0.0 collective-permute-done.2
  22.0 26.3 %collective-permute-done = bf16[4,32,512]{2,1,0:T(8,128)(2,1)} collective-permute-done((bf16[4,32,512]{2,1,0:T(8,128)(2,1)}, bf16[4,32,512]{2,1,0:T(8,128)(2,1)}, u32[]{:S(2)}, u32[]{:S(2)}) %collective-permute-start) | collective-permute-done | bytes 131104 | tf_op jit(solution)/shard_map/ppermute | solution.py:230
  48.3 0.0 collective-permute-done.1
  48.3 0.0 all-to-all-done.x_ref
  48.3 1.8 %shard_map.75 = bf16[1024,384]{1,0:T(8,128)(2,1)S(1)} custom-call(bf16[32,3,32,128]{3,2,1,0:T(8,128)(2,1)S(1)} %all-to-all-done.x_ref, bf16[1024,1024]{1,0:T(8,128)(2,1)S(1)} %shard_map.74.table_ref), custom_call_target="tpu_custom_call" | custom-call | tf_op jit(solution)/shard_map/pallas_call | solution.py:93
  50.1 0.0 copy-start
  50.1 0.9 copy-done
  51.0 18.6 %all-to-all-start.1 = ((bf16[128,8,384]{2,1,0:T(8,128)(2,1)}), bf16[128,8,384]{2,1,0:T(8,128)(2,1)S(1)}, u32[]{:S(2)}, u32[]{:S(2)}) async-start(bf16[128,8,384]{2,1,0:T(8,128)(2,1)} %bitcast.13), calls=%async_computation.1 | async-start | bytes 1572864 | tf_op jit(solution)/shard_map/all_to_all | solution.py:257
  69.6 1.1 pad_maximum_fusion.leg0_ref
  70.7 8.6 %collective-permute-start.5 = (bf16[4,4,32,512]{3,2,1,0:T(8,128)(2,1)S(1)}, bf16[4,4,32,512]{3,2,1,0:T(8,128)(2,1)S(1)}, u32[]{:S(2)}, u32[]{:S(2)}) collective-permute-start(bf16[4,4,32,512]{3,2,1,0:T(8,128)(2,1)S(1)} %pad_maximum_fusion.leg0_ref), channel_id=1, source_target_pairs={{0,384},{1,385},{2,386},{3,387},{4,388},{5,389},{6,390},{7,391},{8... | collective-permute-start | bytes 1572872 | tf_op jit(solution)/shard_map/ppermute | solution.py:230
  79.3 1.9 %collective-permute-start.4 = (bf16[4,4,32,512]{3,2,1,0:T(8,128)(2,1)S(1)}, bf16[4,4,32,512]{3,2,1,0:T(8,128)(2,1)S(1)}, u32[]{:S(2)}, u32[]{:S(2)}) collective-permute-start(bf16[4,4,32,512]{3,2,1,0:T(8,128)(2,1)S(1)} %pad_maximum_fusion.leg0_ref), channel_id=1, source_target_pairs={{0,256},{1,257},{2,258},{3,259},{4,260},{5,261},{6,262},{7,263},{8... | collective-permute-start | bytes 1572872 | tf_op jit(solution)/shard_map/ppermute | solution.py:230
  81.2 2.8 %collective-permute-start.3 = (bf16[4,4,32,512]{3,2,1,0:T(8,128)(2,1)S(1)}, bf16[4,4,32,512]{3,2,1,0:T(8,128)(2,1)S(1)}, u32[]{:S(2)}, u32[]{:S(2)}) collective-permute-start(bf16[4,4,32,512]{3,2,1,0:T(8,128)(2,1)S(1)} %pad_maximum_fusion.leg0_ref), channel_id=1, source_target_pairs={{0,128},{1,129},{2,130},{3,131},{4,132},{5,133},{6,134},{7,135},{8... | collective-permute-start | bytes 1572872 | tf_op jit(solution)/shard_map/ppermute | solution.py:230
  84.0 0.7 fusion
  84.7 0.1 pad_add_fusion.place_ref
  84.8 17.2 %collective-permute-done.5.leg3_ref = bf16[4,4,32,512]{3,2,1,0:T(8,128)(2,1)S(1)} collective-permute-done((bf16[4,4,32,512]{3,2,1,0:T(8,128)(2,1)S(1)}, bf16[4,4,32,512]{3,2,1,0:T(8,128)(2,1)S(1)}, u32[]{:S(2)}, u32[]{:S(2)}) %collective-permute-start.5) | collective-permute-done | bytes 524320 | tf_op jit(solution)/shard_map/ppermute | solution.py:230
  102.0 0.0 collective-permute-done.4.leg2_ref
  102.0 5.6 %collective-permute-done.3.leg1_ref = bf16[4,4,32,512]{3,2,1,0:T(8,128)(2,1)S(1)} collective-permute-done((bf16[4,4,32,512]{3,2,1,0:T(8,128)(2,1)S(1)}, bf16[4,4,32,512]{3,2,1,0:T(8,128)(2,1)S(1)}, u32[]{:S(2)}, u32[]{:S(2)}) %collective-permute-start.3) | collective-permute-done | bytes 524320 | tf_op jit(solution)/shard_map/ppermute | solution.py:230
  107.7 5.1 %all-to-all-done.1 = bf16[128,8,384]{2,1,0:T(8,128)(2,1)S(1)} async-done(((bf16[128,8,384]{2,1,0:T(8,128)(2,1)}), bf16[128,8,384]{2,1,0:T(8,128)(2,1)S(1)}, u32[]{:S(2)}, u32[]{:S(2)}) %all-to-all-start.1) | async-done | bytes 786464 | tf_op jit(solution)/shard_map/all_to_all | solution.py:257
  112.8 2.4 %shard_map.76 = bf16[16,2,32,384]{3,2,1,0:T(8,128)(2,1)S(1)} custom-call(s32[6]{0:T(128)S(1)} %pad_add_fusion.place_ref, bf16[1024,384]{1,0:T(8,128)(2,1)S(1)} %bitcast.14, bf16[4,4,32,512]{3,2,1,0:T(8,128)(2,1)S(1)} %pad_maximum_fusion.leg0_ref, bf16[4,4,32,512]{3,2,1,0:T(8,128)(2,1)S(1)} %collective-permute-done.3.leg1_ref, ...), custom_call_target="tpu_custom_call" | custom-call | tf_op jit(solution)/shard_map/pallas_call | solution.py:150
  115.2 55.9 %all_to_all.15 = bf16[16,2,32,384]{3,2,1,0:T(8,128)(2,1)S(1)} all-to-all(bf16[16,2,32,384]{3,2,1,0:T(8,128)(2,1)S(1)} %shard_map.76), channel_id=1, replica_groups=mesh['x'=4,'zh'=4,'long'=32] {'zh','x'}, dimensions={0} | all-to-all | bytes 1572864 | tf_op jit(solution)/shard_map/all_to_all | solution.py:259
  171.1 0.0 copy-done.2
  171.1 3.3 %shard_map.77 = bf16[8,2,6,32,128]{4,3,2,1,0:T(8,128)(2,1)} custom-call(bf16[4,4,2,32,384]{4,3,2,1,0:T(8,128)(2,1)S(1)} %bitcast.15, bf16[8,2,6,32,128]{4,3,2,1,0:T(8,128)(2,1)S(1)} %bitcast.16, bf16[32,128,128]{2,1,0:T(8,128)(2,1)S(1)} %copy-done.1), custom_call_target="tpu_custom_call" | custom-call | tf_op jit(solution)/shard_map/pallas_call | solution.py:199
  (7 shorter events, 0.0 us)
Async XLA Ops:
  0.0 11.4 %copy-start.3 = (bf16[16,32,512]{2,1,0:T(8,128)(2,1)S(1)}, bf16[16,32,512]{2,1,0:T(8,128)(2,1)}, u32[]{:S(2)}) copy-start(bf16[16,32,512]{2,1,0:T(8,128)(2,1)} %param.10) | copy-start | bytes 1572868
  0.0 16.1 %copy-start.4 = (s32[512]{0:T(512)S(1)}, s32[512]{0:T(512)}, u32[]{:S(2)}) copy-start(s32[512]{0:T(512)} %param.9) | copy-start | bytes 6148
  2.3 46.0 %all-to-all-start = ((bf16[32,3,32,128]{3,2,1,0:T(8,128)(2,1)}), bf16[32,3,32,128]{3,2,1,0:T(8,128)(2,1)S(1)}, u32[]{:S(2)}, u32[]{:S(2)}) async-start(bf16[32,3,32,128]{3,2,1,0:T(8,128)(2,1)} %shard_map.73), calls=%async_computation | async-start | bytes 1572864 | tf_op jit(solution)/shard_map/all_to_all | solution.py:251
  12.2 9.8 %collective-permute-start.2 = (bf16[4,32,512]{2,1,0:T(8,128)(2,1)}, bf16[4,32,512]{2,1,0:T(8,128)(2,1)}, u32[]{:S(2)}, u32[]{:S(2)}) collective-permute-start(bf16[4,32,512]{2,1,0:T(8,128)(2,1)} %get-tuple-element.25), channel_id=1, source_target_pairs={{0,64},{1,65},{2,66},{3,67},{32,96},{33,97},{34,98},{35,99},{36,10... | collective-permute-start | bytes 393224 | tf_op jit(solution)/shard_map/ppermute | solution.py:230
  13.5 34.8 %collective-permute-start = (bf16[4,32,512]{2,1,0:T(8,128)(2,1)}, bf16[4,32,512]{2,1,0:T(8,128)(2,1)}, u32[]{:S(2)}, u32[]{:S(2)}) collective-permute-start(bf16[4,32,512]{2,1,0:T(8,128)(2,1)} %get-tuple-element.26), channel_id=1, source_target_pairs={{0,32},{1,33},{2,34},{3,35},{32,64},{33,65},{34,66},{35,67},{36,68... | collective-permute-start | bytes 393224 | tf_op jit(solution)/shard_map/ppermute | solution.py:230
  14.8 33.5 %collective-permute-start.1 = (bf16[4,32,512]{2,1,0:T(8,128)(2,1)}, bf16[4,32,512]{2,1,0:T(8,128)(2,1)}, u32[]{:S(2)}, u32[]{:S(2)}) collective-permute-start(bf16[4,32,512]{2,1,0:T(8,128)(2,1)} %get-tuple-element.28), channel_id=1, source_target_pairs={{0,96},{1,97},{2,98},{3,99},{32,0},{33,1},{34,2},{35,3},{36,4},{37... | collective-permute-start | bytes 393224 | tf_op jit(solution)/shard_map/ppermute | solution.py:230
  50.1 0.9 copy-start
  51.0 61.8 %all-to-all-start.1 = ((bf16[128,8,384]{2,1,0:T(8,128)(2,1)}), bf16[128,8,384]{2,1,0:T(8,128)(2,1)S(1)}, u32[]{:S(2)}, u32[]{:S(2)}) async-start(bf16[128,8,384]{2,1,0:T(8,128)(2,1)} %bitcast.13), calls=%async_computation.1 | async-start | bytes 1572864 | tf_op jit(solution)/shard_map/all_to_all | solution.py:257
  70.7 31.3 %collective-permute-start.5 = (bf16[4,4,32,512]{3,2,1,0:T(8,128)(2,1)S(1)}, bf16[4,4,32,512]{3,2,1,0:T(8,128)(2,1)S(1)}, u32[]{:S(2)}, u32[]{:S(2)}) collective-permute-start(bf16[4,4,32,512]{3,2,1,0:T(8,128)(2,1)S(1)} %pad_maximum_fusion.leg0_ref), channel_id=1, source_target_pairs={{0,384},{1,385},{2,386},{3,387},{4,388},{5,389},{6,390},{7,391},{8... | collective-permute-start | bytes 1572872 | tf_op jit(solution)/shard_map/ppermute | solution.py:230
  79.3 22.7 %collective-permute-start.4 = (bf16[4,4,32,512]{3,2,1,0:T(8,128)(2,1)S(1)}, bf16[4,4,32,512]{3,2,1,0:T(8,128)(2,1)S(1)}, u32[]{:S(2)}, u32[]{:S(2)}) collective-permute-start(bf16[4,4,32,512]{3,2,1,0:T(8,128)(2,1)S(1)} %pad_maximum_fusion.leg0_ref), channel_id=1, source_target_pairs={{0,256},{1,257},{2,258},{3,259},{4,260},{5,261},{6,262},{7,263},{8... | collective-permute-start | bytes 1572872 | tf_op jit(solution)/shard_map/ppermute | solution.py:230
  81.2 26.4 %collective-permute-start.3 = (bf16[4,4,32,512]{3,2,1,0:T(8,128)(2,1)S(1)}, bf16[4,4,32,512]{3,2,1,0:T(8,128)(2,1)S(1)}, u32[]{:S(2)}, u32[]{:S(2)}) collective-permute-start(bf16[4,4,32,512]{3,2,1,0:T(8,128)(2,1)S(1)} %pad_maximum_fusion.leg0_ref), channel_id=1, source_target_pairs={{0,128},{1,129},{2,130},{3,131},{4,132},{5,133},{6,134},{7,135},{8... | collective-permute-start | bytes 1572872 | tf_op jit(solution)/shard_map/ppermute | solution.py:230
  112.8 58.3 %copy-start.1 = (bf16[32,128,128]{2,1,0:T(8,128)(2,1)S(1)}, bf16[32,128,128]{2,1,0:T(8,128)(2,1)}, u32[]{:S(2)}) copy-start(bf16[32,128,128]{2,1,0:T(8,128)(2,1)} %inverse_ref.1) | copy-start | bytes 3145732
  112.8 58.3 %copy-start.2 = (bf16[16,2,3,32,128]{4,3,2,1,0:T(8,128)(2,1)S(1)}, bf16[16,2,3,32,128]{4,3,2,1,0:T(8,128)(2,1)}, u32[]{:S(2)}) copy-start(bf16[16,2,3,32,128]{4,3,2,1,0:T(8,128)(2,1)} %param.11) | copy-start | bytes 2359300
